TPU v7x, 512 devices: a whole 4x4x16 slice. The times are simulated.
512 devices in a mesh: seq: 128 (over y, z, core), head: 4 (over x).
Axes of the slice: x: 4, y: 4, z: 16, core: 2. Of those that a mesh axis runs over, the one named last changes fastest.
Arguments:
- ids: int32 [256, 256], P('seq'), may hold values from 0 to 32
- pad_mask: int32 [256], P('seq'), may hold values from 0 to 1, as said below
- embed: bfloat16 [33, 768], replicated, may hold values from -16 to 16
- row_qkv: bfloat16 [3, 768, 768], P(None, 'head'), may hold values from -24 to 24
- row_out: bfloat16 [768, 768], P('head'), may hold values from -0.4375 to 0.4375
- col_qkv: bfloat16 [3, 768, 768], P(None, 'head'), may hold values from -24 to 24
- col_out: bfloat16 [768, 768], P('head'), may hold values from -0.21875 to 0.21875
Outputs:
- layer_out: bfloat16 [256, 256, 768], P('seq', None, 'head')
Inputs may be any that keep to these rules, and one draw needn't show every extreme that they name: `pad_mask`: sequence 0 is always real.
All inputs are finite; a program needn't handle non-finite values.
Results may differ from a plain program's by a relative error of at most 0.007.
Values may be sent and summed in bfloat16 or wider, within the bound.
A program may use at most 64 MiB of HBM per device.

v0:
```python
import jax
import jax.numpy as jnp
from jax import lax
from jax.sharding import PartitionSpec as P

HEAD_DIM = 64


EPS = 1e-05


def layer_norm(values):
    mean = jnp.mean(values, axis=-1, keepdims=True)
    centred = values - mean
    spread = jnp.mean(centred * centred, axis=-1, keepdims=True)
    return centred * lax.rsqrt(spread + EPS)


def softmax_last(scores):
    top = jnp.max(scores, axis=-1, keepdims=True)
    weights = jnp.exp(scores - top)
    return weights / jnp.sum(weights, axis=-1, keepdims=True)


def weight_fold(out_weight, piece):
    return jnp.einsum("rce,fe->rcf", piece, out_weight, preferred_element_type=jnp.float32)


def attend_columns(query, keys, values, key_live):
    rows_all, count_cols, local_width = query.shape
    heads_here = local_width // HEAD_DIM
    shape = (rows_all, count_cols, heads_here, HEAD_DIM)
    scores = jnp.einsum(
        "rchd,schd->chrs",
        query.reshape(shape),
        keys.reshape(shape),
        preferred_element_type=jnp.float32,
    ) * HEAD_DIM ** (-0.5)
    scores = jnp.where(key_live > 0, scores, -jnp.inf)
    probs = softmax_last(scores).astype(jnp.bfloat16)
    context = jnp.einsum(
        "chrs,schd->rchd", probs, values.reshape(shape), preferred_element_type=jnp.float32
    )
    return context.astype(jnp.bfloat16).reshape(rows_all, count_cols, local_width)


def send_back(context):
    return lax.all_to_all(context[:, None], "seq", split_axis=0, concat_axis=1, tiled=True)


def body(ids, pad_mask, embed, row_qkv, row_out, col_qkv, col_out):
    rows_here, cols = ids.shape
    width = embed.shape[1]
    local_width = row_out.shape[0]
    heads_here = local_width // HEAD_DIM
    groups = lax.axis_size("seq")
    per_group = cols // groups
    codes = lax.broadcasted_iota(jnp.int32, (1, 1, embed.shape[0]), 2)
    onehot = (ids[:, :, None] == codes).astype(jnp.bfloat16)
    embedded = jnp.einsum("rcv,vd->rcd", onehot, embed, preferred_element_type=jnp.float32)
    normed = layer_norm(embedded).astype(jnp.bfloat16)
    row_proj = jnp.einsum(
        "rcd,ted->trce", normed, row_qkv, preferred_element_type=jnp.float32
    ).astype(jnp.bfloat16)
    live = pad_mask.astype(jnp.bfloat16)
    head_shape = (rows_here, cols, heads_here, HEAD_DIM)
    query = (row_proj[0] * live[:, None, None]).reshape(head_shape)
    keys = row_proj[1].reshape(head_shape)
    values = row_proj[2].reshape(head_shape)
    partial_scores = jnp.einsum("rihd,rjhd->hij", query, keys, preferred_element_type=jnp.float32)
    count_here = jnp.sum(pad_mask.astype(jnp.float32))
    scale = HEAD_DIM ** (-0.5)
    total, count = lax.psum((partial_scores, count_here), "seq")
    row_probs = softmax_last(total * (scale / jnp.sqrt(count))).astype(jnp.bfloat16)
    row_context = jnp.einsum(
        "hij,rjhd->rihd", row_probs, values, preferred_element_type=jnp.float32
    )
    row_context = row_context.astype(jnp.bfloat16).reshape(rows_here, cols, local_width)
    start_feature = lax.axis_index("head") * local_width
    resident = lax.dynamic_slice_in_dim(embedded, start_feature, local_width, 2)
    row_update = weight_fold(row_out, lax.all_gather(row_context, "head", axis=2, tiled=True))
    mixed = resident + row_update
    sums, squares = lax.psum((jnp.sum(mixed, axis=-1), jnp.sum(mixed * mixed, axis=-1)), "head")
    mean = sums / width
    spread = squares / width - mean * mean
    normed_here = ((mixed - mean[..., None]) * lax.rsqrt(spread[..., None] + EPS)).astype(
        jnp.bfloat16
    )
    live_tile = jnp.broadcast_to(live[:, None, None, None], (rows_here, groups, per_group, 1))
    normed_full = lax.all_gather(normed_here, "head", axis=2, tiled=True)
    col_proj = jnp.einsum("rcd,ted->rcte", normed_full, col_qkv, preferred_element_type=jnp.float32)
    packed = col_proj.astype(jnp.bfloat16).reshape(rows_here, groups, per_group, 3 * local_width)
    received = lax.all_to_all(packed, "seq", split_axis=1, concat_axis=0, tiled=True)
    mask_part = lax.all_to_all(live_tile, "seq", split_axis=1, concat_axis=0, tiled=True)
    column_out = send_back(
        attend_columns(
            received[:, 0, :, :local_width],
            received[:, 0, :, local_width : 2 * local_width],
            received[:, 0, :, 2 * local_width :],
            mask_part[:, 0, 0, 0],
        )
    )
    column_out = column_out.reshape(rows_here, cols, local_width)
    col_update = weight_fold(col_out, lax.all_gather(column_out, "head", axis=2, tiled=True))
    return (mixed + col_update).astype(jnp.bfloat16)


def solution(mesh):
    placed = (
        P("seq", None),
        P("seq"),
        P(),
        P(None, "head", None),
        P("head", None),
        P(None, "head", None),
        P("head", None),
    )
    return jax.shard_map(
        body, mesh=mesh, in_specs=placed, out_specs=P("seq", None, "head"), check_vma=False
    )
```

profile of v0, /device:TPU:1, one launch (start us, length us, event | category | flops | bytes accessed | tf_op | source)
XLA Modules:
  0.0 502.3 jit_solution(8825736393220700184)
XLA Ops:
  6.5 1.4 fusion.38
  8.0 0.3 multiply_reduce_fusion
  8.3 0.8 fusion.6
  9.2 1.3 convolution_bitcast_fusion
  10.5 0.6 convert_reduce_fusion
  11.1 0.7 broadcast_in_dim.8
  11.9 20.6 %all-to-all-start.1 = ((bf16[2,128,2,1]{2,0,3,1:T(2,128)(2,1)}), bf16[2,128,2,1]{2,0,3,1:T(2,128)(2,1)S(1)}, u32[]{:S(2)}, u32[]{:S(2)}) async-start(bf16[2,128,2,1]{2,0,3,1:T(2,128)(2,1)} %broadcast_in_dim.8), calls=%async_computation.1 | async-start | bytes 131072 | tf_op jit(solution)/shard_map/all_to_all | solution.py:94
  32.4 248.3 %psum.29 = f32[]{:T(128)} all-reduce(f32[]{:T(128)} %convert_reduce_fusion), channel_id=1, replica_groups=mesh['seq'=128,'head'=4] {'seq'}, use_global_device_ids=true, to_apply=%region_4.0 | all-reduce | flops 1 | bytes 8 | tf_op jit(solution)/shard_map/psum | solution.py:73
  281.4 67.7 %all-reduce.3.cloned.1.call-done = f32[3,256,256]{2,1,0:T(8,128)} async-done(((f32[3,256,256]{2,1,0:T(8,128)}), f32[3,256,256]{2,1,0:T(8,128)}) %all-reduce.3.cloned.1.call-update) | async-done | bytes 786448 | tf_op jit(solution)/shard_map/psum | solution.py:73
  349.1 1.4 fusion.39
  350.6 2.7 fusion.8
  353.3 12.3 %all_gather.9 = bf16[2,256,768]{1,2,0:T(8,128)(2,1)S(1)} all-gather(bf16[2,256,192]{1,2,0:T(8,128)(2,1)S(1)} %bitcast.74), channel_id=1, replica_groups=mesh['seq'=128,'head'=4] {'head'}, dimensions={2}, use_global_device_ids=true | all-gather | bytes 983040 | tf_op jit(solution)/shard_map/all_gather | solution.py:81
  365.5 0.6 fusion.35
  366.2 7.3 %all-reduce = (f32[2,256]{1,0:T(2,128)S(1)}, f32[2,256]{1,0:T(2,128)S(1)}) all-reduce(f32[2,256]{1,0:T(2,128)S(1)} %get-tuple-element.6, f32[2,256]{1,0:T(2,128)S(1)} %get-tuple-element.5), channel_id=1, replica_groups=mesh['seq'=128,'head'=4] {'head'}, use_global_device_ids=true, to_apply=%region_10.0 | all-reduce | flops 1024 | bytes 8192 | tf_op jit(solution)/shard_map/psum | solution.py:83
  373.5 0.2 multiply_convert_fusion.1
  373.9 10.4 %all_gather.10 = bf16[2,256,768]{1,0,2:T(2,128)(2,1)S(1)} all-gather(bf16[2,256,192]{1,0,2:T(2,128)(2,1)S(1)} %copy.60), channel_id=1, replica_groups=mesh['seq'=128,'head'=4] {'head'}, dimensions={2}, use_global_device_ids=true | all-gather | bytes 983040 | tf_op jit(solution)/shard_map/all_gather | solution.py:90
  384.3 1.8 convolution_convert_fusion
  386.1 0.7 copy.62
  386.8 1.1 reshape.40
  387.9 1.3 copy.63
  389.2 20.4 %all-to-all-start = ((bf16[2,128,2,576]{3,2,0,1:T(2,128)(2,1)}), bf16[2,128,2,576]{3,2,0,1:T(2,128)(2,1)S(1)}, u32[]{:S(2)}, u32[]{:S(2)}) async-start(bf16[2,128,2,576]{3,2,0,1:T(2,128)(2,1)} %copy.63), calls=%async_computation | async-start | bytes 1310720 | tf_op jit(solution)/shard_map/all_to_all | solution.py:93
  410.1 37.8 %all-to-all-done = bf16[2,128,2,576]{3,2,0,1:T(2,128)(2,1)S(1)} async-done(((bf16[2,128,2,576]{3,2,0,1:T(2,128)(2,1)}), bf16[2,128,2,576]{3,2,0,1:T(2,128)(2,1)S(1)}, u32[]{:S(2)}, u32[]{:S(2)}) %all-to-all-start) | async-done | bytes 589856 | tf_op jit(solution)/shard_map/all_to_all | solution.py:93
  447.9 0.7 fusion.36
  449.2 1.8 fusion.40
  451.0 1.7 convolution_convert_fusion.3
  452.7 0.2 copy.70
  452.9 30.0 %all_to_all.51 = bf16[256,1,2,192]{3,2,1,0:T(2,128)(2,1)S(1)} all-to-all(bf16[256,1,2,192]{3,2,1,0:T(2,128)(2,1)S(1)} %copy.70), channel_id=1, replica_groups=mesh['seq'=128,'head'=4] {'seq'}, dimensions={0} | all-to-all | bytes 393216 | tf_op jit(solution)/shard_map/all_to_all | solution.py:48
  482.9 0.2 copy.71
  483.1 0.2 copy.72
  483.3 11.0 %all_gather.11 = bf16[2,256,768]{1,2,0:T(8,128)(2,1)S(1)} all-gather(bf16[2,256,192]{1,2,0:T(8,128)(2,1)S(1)} %copy.72), channel_id=1, replica_groups=mesh['seq'=128,'head'=4] {'head'}, dimensions={2}, use_global_device_ids=true | all-gather | bytes 983040 | tf_op jit(solution)/shard_map/all_gather | solution.py:104
  494.3 0.4 fusion.7
  494.7 0.8 copy.74
  (25 shorter events, 1.3 us)
Async XLA Ops:
  6.5 1.8 copy-start
  6.5 342.6 %all-reduce.3.cloned.1.call-start = ((), (), s32[]{:S(2)}) async-start(), calls=%async_computation.3 | async-start | bytes 1572864 | tf_op jit(solution)/shard_map/psum | solution.py:73
  8.3 0.9 copy-start.3
  11.9 377.4 %all-to-all-start.1 = ((bf16[2,128,2,1]{2,0,3,1:T(2,128)(2,1)}), bf16[2,128,2,1]{2,0,3,1:T(2,128)(2,1)S(1)}, u32[]{:S(2)}, u32[]{:S(2)}) async-start(bf16[2,128,2,1]{2,0,3,1:T(2,128)(2,1)} %broadcast_in_dim.8), calls=%async_computation.1 | async-start | bytes 131072 | tf_op jit(solution)/shard_map/all_to_all | solution.py:94
  350.6 15.0 %copy-start.1 = (bf16[192,768]{1,0:T(8,128)(2,1)S(1)}, bf16[192,768]{1,0:T(8,128)(2,1)}, u32[]{:S(2)}) copy-start(bf16[192,768]{1,0:T(8,128)(2,1)} %param.11) | copy-start | bytes 884740
  389.2 58.7 %all-to-all-start = ((bf16[2,128,2,576]{3,2,0,1:T(2,128)(2,1)}), bf16[2,128,2,576]{3,2,0,1:T(2,128)(2,1)S(1)}, u32[]{:S(2)}, u32[]{:S(2)}) async-start(bf16[2,128,2,576]{3,2,0,1:T(2,128)(2,1)} %copy.63), calls=%async_computation | async-start | bytes 1310720 | tf_op jit(solution)/shard_map/all_to_all | solution.py:93
  452.7 41.6 %copy-start.2 = (bf16[192,768]{1,0:T(8,128)(2,1)S(1)}, bf16[192,768]{1,0:T(8,128)(2,1)}, u32[]{:S(2)}) copy-start(bf16[192,768]{1,0:T(8,128)(2,1)} %param.13) | copy-start | bytes 884740
Sparse Core Ops, SparseCore 0:
  10.8 338.2 all-reduce.2
where the time goes:
time: 505 us; the launch traced here: 502 us
  blocking collectives  319 us (63%)
  waiting for transfers between devices  106 us (21%)
  starting transfers between devices  41 us (8%)
  between operations  14.2 us (3%)
  matrix products  12.5 us (2%)
  local copies, waits for them, and re-layouts  7.11 us (1%)
    psum x1, blocking collectives, body(): total, count = lax.psum((partial_scores, count_here), 'seq')  248 us
    psum x1, waiting for transfers between devices, body(): total, count = lax.psum((partial_scores, count_here), 'seq')  67.7 us
    all_to_all x1, waiting for transfers between devices, body(): lax.all_to_all(packed, 'seq', split_axis=1, concat_axis=0, tiled=True)  37.8 us
    all_to_all x1, blocking collectives, send_back(): lax.all_to_all(context[:, None], 'seq', split_axis=0, concat_axis=1, tile...  30 us
    all_to_all x1, starting transfers between devices, body(): lax.all_to_all(live_tile, 'seq', split_axis=1, concat_axis=0, tiled=True)  20.6 us
    all_to_all x1, starting transfers between devices, body(): lax.all_to_all(packed, 'seq', split_axis=1, concat_axis=0, tiled=True)  20.4 us
    all_gather x1, blocking collectives, body(): lax.all_gather(row_context, 'head', axis=2, tiled=True)  12.3 us
    all_gather x1, blocking collectives, body(): lax.all_gather(column_out, 'head', axis=2, tiled=True)  11 us
  transfers between devices with their start and end apart: 3, of which 2 were waited for; matrix products, arithmetic and copies ran while one was open for 2% of the time, Pallas kernels for 0%

commit v1 on v0

v1 whole, which is shorter than its diff:
```python
import jax
import jax.numpy as jnp
from jax import lax
from jax.experimental import pallas as pl
from jax.experimental.pallas import tpu as pltpu
from jax.sharding import PartitionSpec as P

HEAD_DIM = 64
EPS = 1e-05
NX, NY, NZ, NC = 4, 4, 16, 2
VOCAB = 33
D = 768
DH = 192
COLS = 256
ROWS = 256
HP = 16
VH = VOCAB * HP
MESH = pl.DeviceIdType.MESH
F32 = jnp.float32
BF16 = jnp.bfloat16


def dot(a, b, ca=1, cb=0):
    return lax.dot_general(a, b, (((ca,), (cb,)), ((), ())), preferred_element_type=F32)


def norm_rows(values):
    mean = jnp.mean(values, axis=1, keepdims=True)
    centred = values - mean
    spread = jnp.mean(centred * centred, axis=1, keepdims=True)
    return centred * lax.rsqrt(spread + EPS)


def norm_cols(values):
    mean = jnp.mean(values, axis=0, keepdims=True)
    centred = values - mean
    spread = jnp.mean(centred * centred, axis=0, keepdims=True)
    return centred * lax.rsqrt(spread + EPS)


def iota(shape, dim):
    return lax.broadcasted_iota(jnp.int32, shape, dim)


def kernel(
    ids_ref, mask_ref, embed_ref, rqkv_ref, rout_ref, cqkv_ref, cout_ref,
    out_ref,
    idbuf, tab, wro, wco, emb_s, sel_s, qt_s, kf_s, vf_s, kx_s, vxt_s, oh_s, t_s, wm_s,
    mixed_s, ctxs, ctxr, sa, ra, sb,
    zs, zr, ys, yr, ts, tr, ros, ror, rfs, rfr, cos, cor, cfs, cfr, xs, xr, as_, ar, bs, br, ls,
):
    s = lax.axis_index("seq")
    x = lax.axis_index("head")
    y = lax.div(s, NZ * NC)
    z = lax.rem(lax.div(s, NC), NZ)
    core = lax.rem(s, NC)
    grp = y * NC + core
    half = lax.rem(x, 2)
    col_in = lax.div(x, 2)

    def seq_at(yy, zz, cc):
        return (yy * NZ + zz) * NC + cc

    barrier = pltpu.get_barrier_semaphore()

    def greet_line(k, carry):
        pl.semaphore_signal(barrier, inc=1, device_id=(seq_at(y, lax.rem(z + k, NZ), core), x), device_id_type=MESH)
        return carry

    def greet_plane(k, carry):
        place = lax.rem(x * 8 + grp + k, 32)
        px, pg = lax.div(place, 8), lax.rem(place, 8)
        pl.semaphore_signal(
            barrier, inc=1, device_id=(seq_at(lax.div(pg, NC), z, lax.rem(pg, NC)), px), device_id_type=MESH)
        return carry

    lax.fori_loop(1, NZ, greet_line, 0)
    lax.fori_loop(1, 32, greet_plane, 0)

    slot = grp * NZ + z
    m0 = mask_ref[0]
    m1 = mask_ref[1]
    idbuf[slot, :, 0:COLS] = ids_ref[0:1, :] + ids_ref[1:2, :] * 65536
    idbuf[slot, :, COLS:COLS + 128] = jnp.zeros((1, 128), jnp.int32) + (m0 + m1 * 65536)

    pl.semaphore_wait(barrier, NZ - 1 + 31)

    def z_copy(k):
        return pltpu.make_async_remote_copy(
            src_ref=idbuf.at[slot], dst_ref=idbuf.at[slot], send_sem=zs.at[k], recv_sem=zr.at[k],
            device_id=(seq_at(y, lax.rem(z + k, NZ), core), x), device_id_type=MESH)

    def z_arrival(k):
        from_slot = grp * NZ + lax.rem(z + NZ - k, NZ)
        return pltpu.make_async_remote_copy(
            src_ref=idbuf.at[from_slot], dst_ref=idbuf.at[from_slot], send_sem=zs.at[k], recv_sem=zr.at[k],
            device_id=(seq_at(y, lax.rem(z + k, NZ), core), x), device_id_type=MESH)

    def z_start(k, carry):
        z_copy(k).start()
        return carry

    lax.fori_loop(1, NZ, z_start, 0)

    part = pl.ds(pl.multiple_of(core * 96, 96), 96)

    def weight_copy(src, buf, ss, rs, k):
        return pltpu.make_async_remote_copy(
            src_ref=src.at[part, :], dst_ref=buf.at[x, part, :], send_sem=ss.at[k], recv_sem=rs.at[k],
            device_id=(s, lax.rem(x + k, NX)), device_id_type=MESH)

    def weight_arrival(src, buf, ss, rs, k):
        xf = lax.rem(x + NX - k, NX)
        return pltpu.make_async_remote_copy(
            src_ref=src.at[part, :], dst_ref=buf.at[xf, part, :], send_sem=ss.at[k], recv_sem=rs.at[k],
            device_id=(s, lax.rem(x + k, NX)), device_id_type=MESH)

    def forward_copy(buf, ss, rs, k):
        xf = lax.rem(x + NX - k, NX)
        return pltpu.make_async_remote_copy(
            src_ref=buf.at[xf, part, :], dst_ref=buf.at[xf, part, :], send_sem=ss.at[k], recv_sem=rs.at[k],
            device_id=(s + 1 - 2 * core, x), device_id_type=MESH)

    def forward_arrival(buf, ss, rs, k):
        xf = lax.rem(x + NX - k, NX)
        other = pl.ds(pl.multiple_of((1 - core) * 96, 96), 96)
        return pltpu.make_async_remote_copy(
            src_ref=buf.at[xf, other, :], dst_ref=buf.at[xf, other, :], send_sem=ss.at[k], recv_sem=rs.at[k],
            device_id=(s + 1 - 2 * core, x), device_id_type=MESH)

    for k in range(1, NX):
        weight_copy(rout_ref, wro, ros, ror, k).start()

    emb_s[...] = jnp.zeros_like(emb_s)
    emb_s[0:VOCAB, :] = embed_ref[...].astype(F32)
    normed = norm_rows(emb_s[...]).astype(BF16)[0:48, :]
    tab[x] = jnp.zeros((144, 256), BF16)
    for t in range(3):
        tab[x, t * 48:(t + 1) * 48, 0:DH] = dot(normed, rqkv_ref[t], 1, 1).astype(BF16)

    def table_copy(k):
        return pltpu.make_async_remote_copy(
            src_ref=tab.at[x], dst_ref=tab.at[x], send_sem=ts.at[k], recv_sem=tr.at[k],
            device_id=(s, lax.rem(x + k, NX)), device_id_type=MESH)

    def table_arrival(k):
        xf = lax.rem(x + NX - k, NX)
        return pltpu.make_async_remote_copy(
            src_ref=tab.at[xf], dst_ref=tab.at[xf], send_sem=ts.at[k], recv_sem=tr.at[k],
            device_id=(s, lax.rem(x + k, NX)), device_id_type=MESH)

    for k in range(1, NX):
        table_copy(k).start()
    for k in range(1, NX):
        weight_copy(cout_ref, wco, cos, cor, k).start()
    wro[x] = rout_ref[...]
    wco[x] = cout_ref[...]

    emb_t = emb_s[...].T.astype(BF16)
    spot = iota((4 * 256, D), 0)
    goal = lax.div(spot, 256) * DH + lax.rem(spot, 256)
    sel_s[...] = jnp.where(
        jnp.logical_and(goal == iota((4 * 256, D), 1), lax.rem(spot, 256) < DH), 1.0, 0.0).astype(BF16)

    def z_wait(k, carry):
        z_arrival(k).wait_recv()
        return carry

    lax.fori_loop(1, NZ, z_wait, 0)

    def y_copy(k):
        to = lax.rem(grp + k, 8)
        mine = pl.ds(grp * NZ, NZ)
        return pltpu.make_async_remote_copy(
            src_ref=idbuf.at[mine], dst_ref=idbuf.at[mine], send_sem=ys.at[k], recv_sem=yr.at[k],
            device_id=(seq_at(lax.div(to, NC), z, lax.rem(to, NC)), x), device_id_type=MESH)

    def y_arrival(k):
        to = lax.rem(grp + k, 8)
        theirs = pl.ds(lax.rem(grp + 8 - k, 8) * NZ, NZ)
        return pltpu.make_async_remote_copy(
            src_ref=idbuf.at[theirs], dst_ref=idbuf.at[theirs], send_sem=ys.at[k], recv_sem=yr.at[k],
            device_id=(seq_at(lax.div(to, NC), z, lax.rem(to, NC)), x), device_id_type=MESH)

    for k in range(1, 8):
        y_copy(k).start()

    for k in range(1, NX):
        table_arrival(k).wait_recv()
    gathered = jnp.concatenate([tab[i] for i in range(NX)], axis=1)
    tables = dot(gathered, sel_s[...])
    qt_s[...] = jnp.zeros_like(qt_s)
    qt_s[0:48, :] = tables[0:48].astype(BF16)
    kf_s[...] = tables[48:96]
    vf_s[...] = jnp.zeros_like(vf_s)
    vf_s[0:48, :] = tables[96:144]
    own_head = jnp.where(iota((HP, D), 0) == lax.div(iota((HP, D), 1), HEAD_DIM), 1.0, 0.0)

    def expand(b, carry):
        kx_s[pl.ds(pl.multiple_of(b * HP, HP), HP), :] = (kf_s[pl.ds(b, 1), :] * own_head).astype(BF16)
        return carry

    lax.fori_loop(0, VOCAB, expand, 0)
    rep = jnp.where(iota((128, 640), 0) == lax.div(iota((128, 640), 1), HP), 1.0, 0.0).astype(BF16)
    head_of = jnp.where(
        lax.div(iota((D, 640), 0), HEAD_DIM) == lax.rem(iota((D, 640), 1), HP), 1.0, 0.0)
    vxt_s[...] = (dot(vf_s[...].T.astype(BF16), rep) * head_of).astype(BF16)

    for k in range(1, NX):
        weight_arrival(rout_ref, wro, ros, ror, k).wait_recv()
        forward_copy(wro, rfs, rfr, k).start()

    for k in range(1, 8):
        y_arrival(k).wait_recv()

    words = idbuf[:, 0, :]
    low = lax.bitwise_and(words, 65535).astype(F32)
    high = lax.shift_right_logical(words, 16).astype(F32)
    table = jnp.concatenate([low[0:64], high[0:64], low[64:128], high[64:128]], axis=0)
    ids = table[:, 0:COLS].astype(BF16)
    live = table[:, COLS:COLS + 128]
    live2 = jnp.concatenate([live, live], axis=1)
    count = jnp.sum(live2, axis=0, keepdims=True)
    wm_s[0, 0:ROWS, :] = ids

    def onehots(b, carry):
        held = wm_s[0, 0:ROWS, :].astype(F32)
        oh_s[pl.ds(pl.multiple_of(b * ROWS, ROWS), ROWS), :] = jnp.where(
            held == b.astype(F32), 1.0, 0.0).astype(BF16)
        return carry

    lax.fori_loop(0, VOCAB, onehots, 0)

    first_col = z * 16 + grp * 2
    own = []
    for i in range(2):
        pick = jnp.where(iota((128, COLS), 1) == first_col + i, 1.0, 0.0).astype(BF16)
        as_row = dot(pick, ids, 1, 1)
        own.append(jnp.where(as_row == iota((128, ROWS), 0).astype(F32), 1.0, 0.0).astype(BF16))
        pick_t = jnp.where(iota((COLS, 128), 0) == first_col + i, 1.0, 0.0).astype(BF16)
        as_col = dot(ids, pick_t)
        own_t = (jnp.where(as_col == iota((ROWS, 128), 1).astype(F32), 1.0, 0.0) * live).astype(BF16)
        query = dot(own_t, qt_s[...]).astype(BF16)
        score = dot(kx_s[...], query, 1, 1)
        upper = score.astype(BF16)
        lower = (score - upper.astype(F32)).astype(BF16)
        for b in range(VOCAB):
            t_s[i * 32:i * 32 + 16, b * ROWS:(b + 1) * ROWS] = upper[b * HP:(b + 1) * HP]
            t_s[i * 32 + 16:i * 32 + 32, b * ROWS:(b + 1) * ROWS] = lower[b * HP:(b + 1) * HP]

    tied4 = dot(t_s[...], oh_s[...])
    tied = jnp.concatenate([tied4[0:16] + tied4[16:32], tied4[32:48] + tied4[48:64]], axis=0)
    tied = tied * (HEAD_DIM ** (-0.5) * lax.rsqrt(count))
    top = jnp.max(tied, axis=1, keepdims=True)
    weights = jnp.exp(tied - top)
    probs = (weights / jnp.sum(weights, axis=1, keepdims=True)).astype(BF16)

    for b in range(VOCAB):
        share = dot(probs, oh_s[b * ROWS:(b + 1) * ROWS, :], 1, 1)
        wm_s[0, b * HP:(b + 1) * HP, :] = share[0:16].astype(BF16)
        wm_s[1, b * HP:(b + 1) * HP, :] = share[16:32].astype(BF16)

    for k in range(1, NX):
        forward_arrival(wro, rfs, rfr, k).wait_recv()
    row_weight = wro[...].reshape(D, D)
    col_weight = cqkv_ref[...].reshape(3 * DH, D)
    live_here = live2 > 0.0

    def x_copy(to):
        return pltpu.make_async_remote_copy(
            src_ref=ctxs.at[to], dst_ref=ctxr.at[x], send_sem=xs.at[to], recv_sem=xr.at[x],
            device_id=(s, to), device_id_type=MESH)

    def x_arrival(xf):
        return pltpu.make_async_remote_copy(
            src_ref=ctxs.at[xf], dst_ref=ctxr.at[xf], send_sem=xs.at[xf], recv_sem=xr.at[xf],
            device_id=(s, xf), device_id_type=MESH)

    for i in range(2):
        context = dot(vxt_s[:, 0:VH], wm_s[i]).astype(BF16)
        mixed = dot(row_weight, context) + dot(emb_t, own[i])
        mixed_s[2 * i] = mixed[:, 0:128]
        mixed_s[2 * i + 1] = mixed[:, 128:256]
        normed2 = norm_cols(mixed).astype(BF16)
        proj = dot(col_weight, normed2)
        queries = (proj[0:DH].astype(BF16) * jnp.asarray(0.125, BF16))
        keys = jnp.concatenate([proj[DH:2 * DH], jnp.zeros((64, ROWS), F32)], axis=0).T.astype(BF16)
        values = proj[2 * DH:3 * DH].astype(BF16)
        for h in range(3):
            pieces = []
            if h > 0:
                pieces.append(jnp.zeros((64 * h, ROWS), BF16))
            pieces.append(queries[64 * h:64 * h + 64])
            pieces.append(jnp.zeros((256 - 64 * h - 64, ROWS), BF16))
            scores = dot(keys, jnp.concatenate(pieces, axis=0))
            scores = jnp.where(live_here, scores, -1e38)
            raw = jnp.exp(scores - jnp.max(scores, axis=0, keepdims=True))
            total = jnp.sum(raw, axis=0, keepdims=True)
            got = (dot(values[64 * h:64 * h + 64], raw.astype(BF16)) / total).astype(BF16)
            ctxs[2 * i, 64 * h:64 * h + 64, :] = got[:, 0:128]
            ctxs[2 * i + 1, 64 * h:64 * h + 64, :] = got[:, 128:256]
        for to in (2 * i, 2 * i + 1):
            @pl.when(x != to)
            def _():
                x_copy(to).start()

            @pl.when(x == to)
            def _():
                ctxr[to] = ctxs[to]

    for k in range(1, NX):
        weight_arrival(cout_ref, wco, cos, cor, k).wait_recv()
        forward_copy(wco, cfs, cfr, k).start()
    for k in range(1, NX):
        forward_arrival(wco, cfs, cfr, k).wait_recv()
    for xf in range(NX):
        @pl.when(x != xf)
        def _():
            x_arrival(xf).wait_recv()

    done = dot(wco[...].reshape(D, D), ctxr[...].reshape(D, 128)) + mixed_s[x]

    def a_copy(to_x, g):
        to_y = 2 * half + g // 2
        return pltpu.make_async_remote_copy(
            src_ref=sa.at[to_x, g], dst_ref=ra.at[grp * 2 + col_in],
            send_sem=as_.at[to_x * 4 + g], recv_sem=ar.at[grp * 2 + col_in],
            device_id=(seq_at(to_y, z, g % 2), to_x), device_id_type=MESH)

    def a_self(to_x, g):
        return jnp.logical_and(x == to_x, jnp.logical_and(y == 2 * half + g // 2, core == g % 2))

    for to_x in range(NX):
        turned = done[DH * to_x:DH * (to_x + 1)].T
        wide = jnp.concatenate([turned[0:64], turned[64:128]], axis=1).astype(BF16)
        for g in range(4):
            sa[to_x, g] = wide[16 * g:16 * g + 16]
        for g in range(4):
            @pl.when(jnp.logical_not(a_self(to_x, g)))
            def _():
                a_copy(to_x, g).start()

            @pl.when(a_self(to_x, g))
            def _():
                ra[grp * 2 + col_in] = sa[to_x, g]

    def a_from_self(k):
        return jnp.logical_and(grp == k // 2, x == 2 * (k % 2) + lax.div(y, 2))

    def a_arrival(k):
        from_x = 2 * (k % 2) + lax.div(y, 2)
        g = k // 2
        return pltpu.make_async_remote_copy(
            src_ref=ra.at[k], dst_ref=ra.at[k], send_sem=as_.at[k], recv_sem=ar.at[k],
            device_id=(seq_at(g // 2, z, g % 2), from_x), device_id_type=MESH)

    for k in range(16):
        @pl.when(jnp.logical_not(a_from_self(k)))
        def _():
            a_arrival(k).wait_recv()

    order = iota((256, 256), 0)
    swap = jnp.where(lax.rem(order, 16) * 16 + lax.div(order, 16) == iota((256, 256), 1), 1.0, 0.0).astype(BF16)
    sb[...] = dot(swap, ra[...].reshape(256, 384)).astype(BF16)
    place = pl.ds(pl.multiple_of(z * 16, 16), 16)

    def b_copy(k):
        to_z = lax.rem(z + k, NZ)
        return pltpu.make_async_remote_copy(
            src_ref=sb.at[pl.ds(pl.multiple_of(to_z * 16, 16), 16), :], dst_ref=out_ref.at[place, :],
            send_sem=bs.at[k], recv_sem=br.at[k],
            device_id=(seq_at(y, to_z, core), x), device_id_type=MESH)

    def b_arrival(k):
        from_z = lax.rem(z + NZ - k, NZ)
        spot_z = pl.ds(pl.multiple_of(from_z * 16, 16), 16)
        return pltpu.make_async_remote_copy(
            src_ref=sb.at[spot_z, :], dst_ref=out_ref.at[spot_z, :],
            send_sem=bs.at[k], recv_sem=br.at[k],
            device_id=(seq_at(y, lax.rem(z + k, NZ), core), x), device_id_type=MESH)

    def b_start(k, carry):
        b_copy(k).start()
        return carry

    lax.fori_loop(1, NZ, b_start, 0)
    keep = pltpu.make_async_copy(sb.at[place, :], out_ref.at[place, :], ls.at[0])
    keep.start()

    def z_done(k, carry):
        z_copy(k).wait_send()
        return carry

    lax.fori_loop(1, NZ, z_done, 0)
    for k in range(1, 8):
        y_copy(k).wait_send()
    for k in range(1, NX):
        table_copy(k).wait_send()
        weight_copy(rout_ref, wro, ros, ror, k).wait_send()
        weight_copy(cout_ref, wco, cos, cor, k).wait_send()
        forward_copy(wro, rfs, rfr, k).wait_send()
        forward_copy(wco, cfs, cfr, k).wait_send()
    for to in range(NX):
        @pl.when(x != to)
        def _():
            x_copy(to).wait_send()
    for to_x in range(NX):
        for g in range(4):
            @pl.when(jnp.logical_not(a_self(to_x, g)))
            def _():
                a_copy(to_x, g).wait_send()
    keep.wait()

    def b_done(k, carry):
        b_copy(k).wait_send()
        b_arrival(k).wait_recv()
        return carry

    lax.fori_loop(1, NZ, b_done, 0)


def body(ids, pad_mask, embed, row_qkv, row_out, col_qkv, col_out):
    vmem = pl.BlockSpec(memory_space=pltpu.VMEM)
    smem = pl.BlockSpec(memory_space=pltpu.SMEM)
    dma = pltpu.SemaphoreType.DMA
    got = pl.pallas_call(
        kernel,
        out_shape=jax.ShapeDtypeStruct((COLS, 2 * DH), BF16),
        in_specs=[vmem, smem, vmem, vmem, vmem, vmem, vmem],
        out_specs=pl.BlockSpec(memory_space=pl.ANY),
        scratch_shapes=[
            pltpu.VMEM((128, 1, 384), jnp.int32),
            pltpu.VMEM((NX, 144, 256), BF16),
            pltpu.VMEM((NX, DH, D), BF16),
            pltpu.VMEM((NX, DH, D), BF16),
            pltpu.VMEM((128, D), F32),
            pltpu.VMEM((1024, D), BF16),
            pltpu.VMEM((128, D), BF16),
            pltpu.VMEM((48, D), F32),
            pltpu.VMEM((128, D), F32),
            pltpu.VMEM((VH, D), BF16),
            pltpu.VMEM((D, 640), BF16),
            pltpu.VMEM((VOCAB * ROWS, COLS), BF16),
            pltpu.VMEM((64, VOCAB * ROWS), BF16),
            pltpu.VMEM((2, VH, ROWS), BF16),
            pltpu.VMEM((4, D, 128), F32),
            pltpu.VMEM((NX, DH, 128), BF16),
            pltpu.VMEM((NX, DH, 128), BF16),
            pltpu.VMEM((NX, 4, 16, 384), BF16),
            pltpu.VMEM((16, 16, 384), BF16),
            pltpu.VMEM((256, 384), BF16),
            dma((16,)), dma((16,)),
            dma((8,)), dma((8,)),
            dma((4,)), dma((4,)),
            dma((4,)), dma((4,)), dma((4,)), dma((4,)),
            dma((4,)), dma((4,)), dma((4,)), dma((4,)),
            dma((4,)), dma((4,)),
            dma((16,)), dma((16,)),
            dma((16,)), dma((16,)),
            dma((1,)),
        ],
        compiler_params=pltpu.CompilerParams(
            collective_id=0, has_side_effects=True, vmem_limit_bytes=48 * 1024 * 1024),
        cost_estimate=pl.CostEstimate(flops=6_000_000_000, bytes_accessed=4_000_000, transcendentals=500_000),
        name="msa_layer",
    )(ids, pad_mask, embed, row_qkv, row_out, col_qkv, col_out)
    return jnp.transpose(got.reshape(COLS, 2, DH), (1, 0, 2))


def solution(mesh):
    placed = (
        P("seq", None),
        P("seq"),
        P(),
        P(None, "head", None),
        P("head", None),
        P(None, "head", None),
        P("head", None),
    )
    return jax.shard_map(
        body, mesh=mesh, in_specs=placed, out_specs=P("seq", None, "head"), check_vma=False
    )
```

time: 505 us -> 72.7 us (0.14)
  blocking collectives: 319 us -> 0 us
  waiting for transfers between devices: 106 us -> 0 us
  Pallas kernels: 0 us -> 64.9 us
  starting transfers between devices: 41 us -> 0 us
  between operations: 14.2 us -> 0.02 us
  matrix products: 12.5 us -> 0 us
    psum x2 -> x0, blocking collectives: 256 us -> none  [the longest x1 248 us: body(): total, count = lax.psum((partial_scores, count_here), 'seq')]
    psum x1 -> x0, waiting for transfers between devices: 67.7 us -> none  [body(): total, count = lax.psum((partial_scores, count_here), 'seq')]
    pallas_call x0 -> x1, Pallas kernels: none -> 64.9 us  [body(): pl.pallas_call(kernel, out_shape=jax.ShapeDtypeStruct((COLS, 2 * DH), BF1...]
    all_to_all x2 -> x0, starting transfers between devices: 41 us -> none  [the longest x1 20.6 us: body(): lax.all_to_all(live_tile, 'seq', split_axis=1, concat_axis=0, tiled=True)]
    all_to_all x2 -> x0, waiting for transfers between devices: 37.8 us -> none  [the longest x1 37.8 us: body(): lax.all_to_all(packed, 'seq', split_axis=1, concat_axis=0, tiled=True)]
    all_gather x3 -> x0, blocking collectives: 33.7 us -> none  [the longest x1 12.3 us: body(): lax.all_gather(row_context, 'head', axis=2, tiled=True)]
    all_to_all x1 -> x0, blocking collectives: 30 us -> none  [send_back(): lax.all_to_all(context[:, None], 'seq', split_axis=0, concat_axis=1, tile...]
    dot_general x8 -> x0, matrix products: 10.7 us -> none  [the longest x1 2.66 us: body(): jnp.einsum('hij,rjhd->rihd', row_probs, values, preferred_element_type=jn...]
  transfers between devices with their start and end apart: 3 -> 0, of which waited for: 2 -> 0; matrix products, arithmetic and copies ran while one was open for 2% -> 0% of each run, Pallas kernels for 0% -> 0%
where the time goes in v1:
time: 72.7 us; the launch traced here: 72.2 us
  Pallas kernels  64.9 us (89%)
  local copies, waits for them, and re-layouts  7.24 us (10%)
    pallas_call x1, Pallas kernels, body(): pl.pallas_call(kernel, out_shape=jax.ShapeDtypeStruct((COLS, 2 * DH), BF1...  64.9 us
    unnamed x14, local copies, waits for them, and re-layouts  6.42 us

profile of v1, /device:TPU:1, one launch (start us, length us, event | category | flops | bytes accessed | tf_op | source)
XLA Modules:
  0.0 72.2 jit_solution(8024712491690172536)
XLA Ops:
  0.0 0.0 copy-start
  0.0 1.2 %copy-done = bf16[3,192,768]{2,1,0:T(8,128)(2,1)S(1)} copy-done((bf16[3,192,768]{2,1,0:T(8,128)(2,1)S(1)}, bf16[3,192,768]{2,1,0:T(8,128)(2,1)}, u32[]{:S(2)}) %copy-start) | copy-done | bytes 884760
  1.2 0.0 copy-start.1
  1.2 1.2 %copy-done.1 = bf16[3,192,768]{2,1,0:T(8,128)(2,1)S(1)} copy-done((bf16[3,192,768]{2,1,0:T(8,128)(2,1)S(1)}, bf16[3,192,768]{2,1,0:T(8,128)(2,1)}, u32[]{:S(2)}) %copy-start.1) | copy-done | bytes 884760
  2.3 0.0 copy-start.2
  2.3 1.0 %copy-done.2 = bf16[192,768]{1,0:T(8,128)(2,1)S(1)} copy-done((bf16[192,768]{1,0:T(8,128)(2,1)S(1)}, bf16[192,768]{1,0:T(8,128)(2,1)}, u32[]{:S(2)}) %copy-start.2) | copy-done | bytes 294936
  3.3 0.0 copy-start.3
  3.3 1.0 %copy-done.3 = bf16[192,768]{1,0:T(8,128)(2,1)S(1)} copy-done((bf16[192,768]{1,0:T(8,128)(2,1)S(1)}, bf16[192,768]{1,0:T(8,128)(2,1)}, u32[]{:S(2)}) %copy-start.3) | copy-done | bytes 294936
  4.3 0.0 copy-start.4
  4.3 0.8 %copy-done.4 = bf16[33,768]{1,0:T(8,128)(2,1)S(1)} copy-done((bf16[33,768]{1,0:T(8,128)(2,1)S(1)}, bf16[33,768]{1,0:T(8,128)(2,1)}, u32[]{:S(2)}) %copy-start.4) | copy-done | bytes 50712
  5.1 0.0 copy-start.5
  5.1 0.7 copy-done.5
  5.8 0.0 copy-start.6
  5.8 0.7 copy-done.6
  6.4 64.9 %msa_layer.1 = bf16[256,384]{1,0:T(8,128)(2,1)S(1)} custom-call(s32[2,256]{1,0:T(2,128)S(1)} %copy-done.5, s32[2]{0:T(128)S(1)} %copy-done.6, bf16[33,768]{1,0:T(8,128)(2,1)S(1)} %copy-done.4, bf16[3,192,768]{2,1,0:T(8,128)(2,1)S(1)} %copy-done, bf16[192,768]{1,0:T(8,128)(2,1)S(1)} %copy-done.2, bf16[3,192,768]{2,1,0:T(8,128)(2,1)S(1)} %copy-done.1, ...), custom_call_target="tpu_custom_call" | custom-call | flops 6000000000 | bytes 4000000 | tf_op jit(solution)/shard_map/msa_layer/pallas_call | solution.py:426
  71.4 0.8 %copy.9 = bf16[256,384]{0,1:T(8,128)(2,1)} copy(bf16[256,384]{1,0:T(8,128)(2,1)S(1)} %msa_layer.1) | data formatting | bytes 393216 | tf_op jit(solution)/shard_map/msa_layer/pallas_call | solution.py:426
Async XLA Ops:
  0.0 1.2 %copy-start = (bf16[3,192,768]{2,1,0:T(8,128)(2,1)S(1)}, bf16[3,192,768]{2,1,0:T(8,128)(2,1)}, u32[]{:S(2)}) copy-start(bf16[3,192,768]{2,1,0:T(8,128)(2,1)} %rqkv_ref.1) | copy-start | bytes 2654212
  1.2 1.2 %copy-start.1 = (bf16[3,192,768]{2,1,0:T(8,128)(2,1)S(1)}, bf16[3,192,768]{2,1,0:T(8,128)(2,1)}, u32[]{:S(2)}) copy-start(bf16[3,192,768]{2,1,0:T(8,128)(2,1)} %cqkv_ref.1) | copy-start | bytes 2654212
  2.3 1.0 %copy-start.2 = (bf16[192,768]{1,0:T(8,128)(2,1)S(1)}, bf16[192,768]{1,0:T(8,128)(2,1)}, u32[]{:S(2)}) copy-start(bf16[192,768]{1,0:T(8,128)(2,1)} %rout_ref.1) | copy-start | bytes 884740
  3.3 1.0 %copy-start.3 = (bf16[192,768]{1,0:T(8,128)(2,1)S(1)}, bf16[192,768]{1,0:T(8,128)(2,1)}, u32[]{:S(2)}) copy-start(bf16[192,768]{1,0:T(8,128)(2,1)} %cout_ref.1) | copy-start | bytes 884740
  4.3 0.8 %copy-start.4 = (bf16[33,768]{1,0:T(8,128)(2,1)S(1)}, bf16[33,768]{1,0:T(8,128)(2,1)}, u32[]{:S(2)}) copy-start(bf16[33,768]{1,0:T(8,128)(2,1)} %embed_ref.1) | copy-start | bytes 152068
  5.1 0.7 copy-start.5
  5.8 0.7 copy-start.6

commit v2 on v1

v2 whole, which is shorter than its diff:
```python
import jax
import jax.numpy as jnp
from jax import lax
from jax.experimental import pallas as pl
from jax.experimental.pallas import tpu as pltpu
from jax.sharding import PartitionSpec as P

HEAD_DIM = 64
EPS = 1e-05
NX, NY, NZ, NC = 4, 4, 16, 2
VOCAB = 33
D = 768
DH = 192
COLS = 256
ROWS = 256
HP = 16
VH = VOCAB * HP
FAR_Z = (8, 9, 7, 10, 6, 11, 5, 12, 4, 13, 3, 14, 2, 15, 1)
FAR_Y = (4, 5, 3, 2, 6, 7, 1)
FAR_X = (2, 1, 3)
FAR_PLANE = (10, 11, 8, 9, 6, 7, 14, 15, 4, 5, 12, 13, 2, 3, 1, 0)
MESH = pl.DeviceIdType.MESH
F32 = jnp.float32
BF16 = jnp.bfloat16


def dot(a, b, ca=1, cb=0):
    return lax.dot_general(a, b, (((ca,), (cb,)), ((), ())), preferred_element_type=F32)


def norm_rows(values):
    mean = jnp.mean(values, axis=1, keepdims=True)
    centred = values - mean
    spread = jnp.mean(centred * centred, axis=1, keepdims=True)
    return centred * lax.rsqrt(spread + EPS)


def norm_cols(values):
    mean = jnp.mean(values, axis=0, keepdims=True)
    centred = values - mean
    spread = jnp.mean(centred * centred, axis=0, keepdims=True)
    return centred * lax.rsqrt(spread + EPS)


def iota(shape, dim):
    return lax.broadcasted_iota(jnp.int32, shape, dim)


class Exchange:
    opened = []

    def __init__(self, out, into, keys, sends=None, arrives=None):
        self.out, self.into, self.keys = out, into, keys
        self.sends = sends or (lambda k: None)
        self.arrives = arrives or (lambda k: None)
        Exchange.opened.append(self)
        self.waited = False

    def each(self, run, keys=None):
        for k in self.keys if keys is None else keys:
            run(k)

    def start(self, keys=None):
        def run(k):
            gate(self.sends(k), lambda: self.out(k).start())
        self.each(run, keys)

    def receive(self, keys=None):
        self.waited = True

        def run(k):
            gate(self.arrives(k), lambda: self.into(k).wait_recv())
        self.each(run, keys)

    def finish(self):
        def run(k):
            gate(self.sends(k), lambda: self.out(k).wait_send())
        self.each(run)


def gate(condition, action):
    if condition is None:
        action()
    else:
        pl.when(condition)(action)


def kernel(
    ids_hbm, mask_hbm, embed_hbm, rqkv_hbm, rout_hbm, cqkv_hbm, cout_hbm,
    out_ref,
    ids_ref, mask_ref, embed_ref, rqkv_ref, cqkv_ref,
    idbuf, tab, wro, wco, emb_s, sel_s, qt_s, kf_s, vf_s, kx_s, vxt_s, wm_s, sc_s,
    mixed_s, ctxs, ctxr, sa, ra, sb,
    zs, zr, ys, yr, ts, tr, ros, ror, rfs, rfr, cos, cor, cfs, cfr, xs, xr, as_, ar, bs, br, ls,
):
    Exchange.opened = []
    s = lax.axis_index("seq")
    x = lax.axis_index("head")
    y = lax.div(s, NZ * NC)
    z = lax.rem(lax.div(s, NC), NZ)
    core = lax.rem(s, NC)
    grp = y * NC + core
    half = lax.rem(x, 2)
    col_in = lax.div(x, 2)

    def seq_at(yy, zz, cc):
        return (yy * NZ + zz) * NC + cc

    def remote(src, dst, ss, rs, to_s, to_x):
        return pltpu.make_async_remote_copy(
            src_ref=src, dst_ref=dst, send_sem=ss, recv_sem=rs, device_id=(to_s, to_x), device_id_type=MESH)

    barrier = pltpu.get_barrier_semaphore()

    def greet_line(k, carry):
        pl.semaphore_signal(barrier, inc=1, device_id=(seq_at(y, lax.rem(z + k, NZ), core), x), device_id_type=MESH)
        return carry

    def greet_plane(k, carry):
        place = lax.rem(x * 8 + grp + k, 32)
        px, pg = lax.div(place, 8), lax.rem(place, 8)
        pl.semaphore_signal(
            barrier, inc=1, device_id=(seq_at(lax.div(pg, NC), z, lax.rem(pg, NC)), px), device_id_type=MESH)
        return carry

    lax.fori_loop(1, NZ, greet_line, 0)
    lax.fori_loop(1, 32, greet_plane, 0)
    fetch = [
        pltpu.make_async_copy(a, b, ls.at[i]) for i, (a, b) in enumerate((
            (ids_hbm, ids_ref), (mask_hbm, mask_ref), (embed_hbm, embed_ref), (rqkv_hbm, rqkv_ref),
            (rout_hbm, wro.at[x]), (cqkv_hbm, cqkv_ref), (cout_hbm, wco.at[x])))
    ]
    for copy in fetch:
        copy.start()

    slot = grp * NZ + z
    fetch[0].wait()
    fetch[1].wait()
    m0 = mask_ref[0]
    m1 = mask_ref[1]
    idbuf[slot, :, 0:COLS] = ids_ref[0:1, :] + ids_ref[1:2, :] * 65536
    idbuf[slot, :, COLS:COLS + 128] = jnp.zeros((1, 128), jnp.int32) + (m0 + m1 * 65536)

    fetch[2].wait()
    emb_s[...] = jnp.zeros_like(emb_s)
    emb_s[0:VOCAB, :] = embed_ref[...].astype(F32)
    normed = norm_rows(emb_s[...]).astype(BF16)[0:48, :]
    tab[x] = jnp.zeros((144, 256), BF16)
    fetch[3].wait()
    for t in range(3):
        tab[x, t * 48:(t + 1) * 48, 0:DH] = dot(normed, rqkv_ref[t], 1, 1).astype(BF16)

    pl.semaphore_wait(barrier, NZ - 1 + 31)

    def z_slot(k):
        return idbuf.at[grp * NZ + lax.rem(z + NZ - k, NZ)]

    ids_z = Exchange(
        lambda k: remote(idbuf.at[slot], idbuf.at[slot], zs.at[k], zr.at[k], seq_at(y, lax.rem(z + k, NZ), core), x),
        lambda k: remote(z_slot(k), z_slot(k), zs.at[k], zr.at[k], seq_at(y, lax.rem(z + k, NZ), core), x),
        FAR_Z)
    ids_z.start()

    part = pl.ds(pl.multiple_of(core * 96, 96), 96)
    other = pl.ds(pl.multiple_of((1 - core) * 96, 96), 96)
    ahead = lambda k: lax.rem(x + k, NX)
    behind = lambda k: lax.rem(x + NX - k, NX)

    def weight(src, buf, ss, rs):
        return Exchange(
            lambda k: remote(src.at[part, :], buf.at[x, part, :], ss.at[k], rs.at[k], s, ahead(k)),
            lambda k: remote(src.at[part, :], buf.at[behind(k), part, :], ss.at[k], rs.at[k], s, ahead(k)),
            FAR_X)

    def forward(buf, ss, rs):
        twin = s + 1 - 2 * core
        return Exchange(
            lambda k: remote(
                buf.at[behind(k), part, :], buf.at[behind(k), part, :], ss.at[k], rs.at[k], twin, x),
            lambda k: remote(
                buf.at[behind(k), other, :], buf.at[behind(k), other, :], ss.at[k], rs.at[k], twin, x),
            FAR_X)

    tabs = Exchange(
        lambda k: remote(tab.at[x], tab.at[x], ts.at[k], tr.at[k], s, ahead(k)),
        lambda k: remote(tab.at[behind(k)], tab.at[behind(k)], ts.at[k], tr.at[k], s, ahead(k)),
        FAR_X)
    tabs.start()
    row_out = weight(rout_hbm, wro, ros, ror)
    row_out.start()
    col_out = weight(cout_hbm, wco, cos, cor)

    emb_t = emb_s[...].T.astype(BF16)
    spot = iota((4 * 256, D), 0)
    goal = lax.div(spot, 256) * DH + lax.rem(spot, 256)
    sel_s[...] = jnp.where(
        jnp.logical_and(goal == iota((4 * 256, D), 1), lax.rem(spot, 256) < DH), 1.0, 0.0).astype(BF16)

    ids_z.receive()
    mine = pl.ds(grp * NZ, NZ)

    def y_seq(k):
        to = lax.rem(grp + k, 8)
        return seq_at(lax.div(to, NC), z, lax.rem(to, NC))

    def y_part(k):
        return idbuf.at[pl.ds(lax.rem(grp + 8 - k, 8) * NZ, NZ)]

    ids_y = Exchange(
        lambda k: remote(idbuf.at[mine], idbuf.at[mine], ys.at[k], yr.at[k], y_seq(k), x),
        lambda k: remote(y_part(k), y_part(k), ys.at[k], yr.at[k], y_seq(k), x),
        FAR_Y)
    ids_y.start()
    col_out.start()

    tabs.receive()
    gathered = jnp.concatenate([tab[i] for i in range(NX)], axis=1)
    tables = dot(gathered, sel_s[...])
    qt_s[...] = jnp.zeros_like(qt_s)
    qt_s[0:48, :] = tables[0:48].astype(BF16)
    kf_s[...] = tables[48:96]
    vf_s[...] = jnp.zeros_like(vf_s)
    vf_s[0:48, :] = tables[96:144]
    own_head = jnp.where(iota((HP, D), 0) == lax.div(iota((HP, D), 1), HEAD_DIM), 1.0, 0.0)

    def expand(b, carry):
        kx_s[pl.ds(pl.multiple_of(b * HP, HP), HP), :] = (kf_s[pl.ds(b, 1), :] * own_head).astype(BF16)
        return carry

    lax.fori_loop(0, VOCAB, expand, 0)
    scores_of = dot(kx_s[...], qt_s[...], 1, 1)
    upper = scores_of.astype(BF16)
    sc_s[0:VH, :] = upper
    sc_s[VH:2 * VH, :] = (scores_of - upper.astype(F32)).astype(BF16)
    rep = jnp.where(iota((128, 640), 0) == lax.div(iota((128, 640), 1), HP), 1.0, 0.0).astype(BF16)
    head_of = jnp.where(
        lax.div(iota((D, 640), 0), HEAD_DIM) == lax.rem(iota((D, 640), 1), HP), 1.0, 0.0)
    vxt_s[...] = (dot(vf_s[...].T.astype(BF16), rep) * head_of).astype(BF16)

    ids_y.receive()
    row_share = forward(wro, rfs, rfr)
    row_out.receive()
    row_share.start()

    words = idbuf[:, 0, :]
    low = lax.bitwise_and(words, 65535).astype(F32)
    high = lax.shift_right_logical(words, 16).astype(F32)
    table = jnp.concatenate([low[0:64], high[0:64], low[64:128], high[64:128]], axis=0)
    ids = table[:, 0:COLS].astype(BF16)
    live = table[:, COLS:COLS + 128]
    live2 = jnp.concatenate([live, live], axis=1)
    eye = jnp.where(iota((COLS, COLS), 0) == iota((COLS, COLS), 1), 1.0, 0.0).astype(BF16)
    ids_t = dot(eye, ids, 1, 1).astype(BF16)

    def onehot(of, b):
        return jnp.where(of == jnp.asarray(b, BF16), jnp.asarray(1, BF16), jnp.asarray(0, BF16))

    count = jnp.sum(live2, axis=0, keepdims=True)
    first_col = z * 16 + grp * 2
    token = iota((128, ROWS), 0).astype(F32)
    first_lane = jnp.where(iota((128, 128), 1) == 0, 1.0, 0.0).astype(BF16)
    live_row = dot(first_lane, live.astype(BF16), 1, 1)
    own, own_live = [], []
    for i in range(2):
        pick = jnp.where(iota((128, COLS), 1) == first_col + i, 1.0, 0.0).astype(BF16)
        hit = jnp.where(dot(pick, ids, 1, 1) == token, 1.0, 0.0)
        own.append(hit.astype(BF16))
        own_live.append((hit * live_row).astype(BF16))
    own = jnp.concatenate(own, axis=1)
    picked = dot(sc_s[...], jnp.concatenate(own_live, axis=1)).astype(BF16)
    sums = [None] * 4
    for b in range(VOCAB):
        left = jnp.concatenate([
            picked[b * HP:(b + 1) * HP, 0:ROWS], picked[VH + b * HP:VH + (b + 1) * HP, 0:ROWS],
            picked[b * HP:(b + 1) * HP, ROWS:], picked[VH + b * HP:VH + (b + 1) * HP, ROWS:]], axis=0)
        term = dot(left, onehot(ids, b))
        sums[b % 4] = term if sums[b % 4] is None else sums[b % 4] + term
    tied4 = (sums[0] + sums[1]) + (sums[2] + sums[3])
    tied = jnp.concatenate([tied4[0:16] + tied4[16:32], tied4[32:48] + tied4[48:64]], axis=0)
    tied = tied * (HEAD_DIM ** (-0.5) * lax.rsqrt(count))
    top = jnp.max(tied, axis=1, keepdims=True)
    weights = jnp.exp(tied - top)
    probs = (weights / jnp.sum(weights, axis=1, keepdims=True)).astype(BF16)

    for b in range(VOCAB):
        share = dot(probs, onehot(ids_t, b))
        wm_s[b * HP:(b + 1) * HP, 0:ROWS] = share[0:16].astype(BF16)
        wm_s[b * HP:(b + 1) * HP, ROWS:2 * ROWS] = share[16:32].astype(BF16)

    fetch[4].wait()
    fetch[5].wait()
    row_share.receive()
    row_weight = wro[...].reshape(D, D)
    col_weight = cqkv_ref[...].reshape(3 * DH, D)
    live_here = live2 > 0.0

    context = dot(vxt_s[:, 0:VH], wm_s[...]).astype(BF16)
    mixed = dot(row_weight, context) + dot(emb_t, own)
    for q in range(4):
        mixed_s[q] = mixed[:, 128 * q:128 * q + 128]
    proj = dot(col_weight, norm_cols(mixed).astype(BF16))
    scores, values = [], []
    for i in range(2):
        at = slice(i * ROWS, (i + 1) * ROWS)
        query = proj[0:DH, at].astype(BF16) * jnp.asarray(0.125, BF16)
        key = proj[DH:2 * DH, at].astype(BF16)
        value = proj[2 * DH:3 * DH, at].astype(BF16)
        for h in range(0, DH, HEAD_DIM):
            scores.append(dot(key[h:h + HEAD_DIM], query[h:h + HEAD_DIM], 0, 0))
            values.append(value[h:h + HEAD_DIM])
    weighted, totals = [], []
    for score in scores:
        score = jnp.where(live_here, score, -1e38)
        raw = jnp.exp(score - jnp.max(score, axis=0, keepdims=True))
        totals.append(1.0 / jnp.sum(raw, axis=0, keepdims=True))
        weighted.append(raw.astype(BF16))
    for q in range(6):
        got = (dot(values[q], weighted[q]) * totals[q]).astype(BF16)
        at = slice((q % 3) * HEAD_DIM, (q % 3 + 1) * HEAD_DIM)
        ctxs[q // 3 * 2, at, :] = got[:, 0:128]
        ctxs[q // 3 * 2 + 1, at, :] = got[:, 128:256]
    to_slot = Exchange(
        lambda k: remote(ctxs.at[ahead(k)], ctxr.at[x], xs.at[k], xr.at[k], s, ahead(k)),
        lambda k: remote(ctxs.at[ahead(k)], ctxr.at[behind(k)], xs.at[k], xr.at[k], s, ahead(k)),
        FAR_X)
    to_slot.start()
    col_share = forward(wco, cfs, cfr)
    col_out.receive()
    col_share.start()
    ctxr[x] = ctxs[x]

    fetch[6].wait()
    col_share.receive()
    to_slot.receive()

    done = dot(wco[...].reshape(D, D), ctxr[...].reshape(D, 128)) + mixed_s[x]

    def a_place(j):
        to_x = lax.rem(x + j // 4, NX)
        to_half = lax.rem(y + (j // 2) % 2, 2)
        return to_x, to_half, lax.rem(core + j % 2, 2)

    def a_out(j):
        to_x, to_half, to_core = a_place(j)
        k = grp * 2 + col_in
        return remote(
            sa.at[to_x, to_half * 2 + to_core], ra.at[k], as_.at[j], ar.at[k],
            seq_at(2 * half + to_half, z, to_core), to_x)

    def a_into(j):
        from_y = lax.rem(y + j // 4, NY)
        from_core = lax.rem(core + j % 2, 2)
        from_col = lax.rem(col_in + (j // 2) % 2, 2)
        k = (from_y * NC + from_core) * 2 + from_col
        return remote(
            ra.at[k], ra.at[k], as_.at[j], ar.at[k], seq_at(from_y, z, from_core), 2 * from_col + lax.div(y, 2))

    stays = half == lax.div(y, 2)
    to_plane = Exchange(
        a_out, a_into, FAR_PLANE,
        lambda j: jnp.logical_not(stays) if j == 0 else None,
        lambda j: jnp.logical_not(stays) if j == 0 else None)
    for to_x in range(NX):
        turned = done[DH * to_x:DH * (to_x + 1)].T
        wide = jnp.concatenate([turned[0:64], turned[64:128]], axis=1).astype(BF16)
        for g in range(4):
            sa[to_x, g] = wide[16 * g:16 * g + 16]
    to_plane.start()

    @pl.when(stays)
    def _():
        ra[grp * 2 + col_in] = sa[x, lax.rem(y, 2) * 2 + core]

    order = iota((256, 256), 0)
    swap = jnp.where(lax.rem(order, 16) * 16 + lax.div(order, 16) == iota((256, 256), 1), 1.0, 0.0).astype(BF16)
    to_plane.receive()

    sb[...] = dot(swap, ra[...].reshape(256, 384)).astype(BF16)

    def z_rows(at):
        return pl.ds(pl.multiple_of(at * 16, 16), 16)

    to_rows = Exchange(
        lambda k: remote(
            sb.at[z_rows(lax.rem(z + k, NZ)), :], out_ref.at[z_rows(z), :], bs.at[k], br.at[k],
            seq_at(y, lax.rem(z + k, NZ), core), x),
        lambda k: remote(
            sb.at[z_rows(lax.rem(z + NZ - k, NZ)), :], out_ref.at[z_rows(lax.rem(z + NZ - k, NZ)), :],
            bs.at[k], br.at[k], seq_at(y, lax.rem(z + k, NZ), core), x),
        tuple(range(1, NZ)))
    to_rows.start()
    keep = pltpu.make_async_copy(sb.at[z_rows(z), :], out_ref.at[z_rows(z), :], ls.at[7])
    keep.start()

    ids_z.finish()
    ids_y.finish()
    tabs.finish()
    for weights_sent in (row_out, col_out, row_share, col_share):
        weights_sent.finish()
    to_slot.finish()
    to_plane.finish()
    keep.wait()
    to_rows.receive()
    to_rows.finish()


def body(ids, pad_mask, embed, row_qkv, row_out, col_qkv, col_out):
    dma = pltpu.SemaphoreType.DMA
    got = pl.pallas_call(
        kernel,
        out_shape=jax.ShapeDtypeStruct((COLS, 2 * DH), BF16),
        in_specs=[pl.BlockSpec(memory_space=pltpu.HBM)] * 7,
        out_specs=pl.BlockSpec(memory_space=pl.ANY),
        scratch_shapes=[
            pltpu.VMEM((2, COLS), jnp.int32),
            pltpu.SMEM((2,), jnp.int32),
            pltpu.VMEM((VOCAB, D), BF16),
            pltpu.VMEM((3, DH, D), BF16),
            pltpu.VMEM((3, DH, D), BF16),
            pltpu.VMEM((128, 1, 384), jnp.int32),
            pltpu.VMEM((NX, 144, 256), BF16),
            pltpu.VMEM((NX, DH, D), BF16),
            pltpu.VMEM((NX, DH, D), BF16),
            pltpu.VMEM((128, D), F32),
            pltpu.VMEM((1024, D), BF16),
            pltpu.VMEM((128, D), BF16),
            pltpu.VMEM((48, D), F32),
            pltpu.VMEM((128, D), F32),
            pltpu.VMEM((VH, D), BF16),
            pltpu.VMEM((D, 640), BF16),
            pltpu.VMEM((VH, 2 * ROWS), BF16),
            pltpu.VMEM((2 * VH, 128), BF16),
            pltpu.VMEM((4, D, 128), F32),
            pltpu.VMEM((NX, DH, 128), BF16),
            pltpu.VMEM((NX, DH, 128), BF16),
            pltpu.VMEM((NX, 4, 16, 384), BF16),
            pltpu.VMEM((16, 16, 384), BF16),
            pltpu.VMEM((256, 384), BF16),
            dma((16,)), dma((16,)),
            dma((8,)), dma((8,)),
            dma((4,)), dma((4,)),
            dma((4,)), dma((4,)), dma((4,)), dma((4,)),
            dma((4,)), dma((4,)), dma((4,)), dma((4,)),
            dma((4,)), dma((4,)),
            dma((16,)), dma((16,)),
            dma((16,)), dma((16,)),
            dma((8,)),
        ],
        compiler_params=pltpu.CompilerParams(
            collective_id=0, has_side_effects=True, vmem_limit_bytes=63 * 1024 * 1024),
        cost_estimate=pl.CostEstimate(flops=6_000_000_000, bytes_accessed=4_000_000, transcendentals=500_000),
        name="msa_layer",
    )(ids, pad_mask, embed, row_qkv, row_out, col_qkv, col_out)
    return jnp.transpose(got.reshape(COLS, 2, DH), (1, 0, 2))


def solution(mesh):
    placed = (
        P("seq", None),
        P("seq"),
        P(),
        P(None, "head", None),
        P("head", None),
        P(None, "head", None),
        P("head", None),
    )
    return jax.shard_map(
        body, mesh=mesh, in_specs=placed, out_specs=P("seq", None, "head"), check_vma=False
    )
```

time: 72.7 us -> 61.6 us (0.85)
  Pallas kernels: 64.9 us -> 59.3 us
  local copies, waits for them, and re-layouts: 7.24 us -> 1.74 us
    unnamed x14 -> x0, local copies, waits for them, and re-layouts: 6.42 us -> none
    pallas_call x1, Pallas kernels: 64.9 us -> 59.3 us  [body(): pl.pallas_call(kernel, out_shape=jax.ShapeDtypeStruct((COLS, 2 * DH), BF1...]
    pallas_call x1, local copies, waits for them, and re-layouts: 0.82 us -> 1.74 us  [body(): pl.pallas_call(kernel, out_shape=jax.ShapeDtypeStruct((COLS, 2 * DH), BF1...]
where the time goes in v2:
time: 61.6 us; the launch traced here: 61 us
  Pallas kernels  59.3 us (96%)
  local copies, waits for them, and re-layouts  1.74 us (3%)
    pallas_call x1, Pallas kernels, body(): pl.pallas_call(kernel, out_shape=jax.ShapeDtypeStruct((COLS, 2 * DH), BF1...  59.3 us
    pallas_call x1, local copies, waits for them, and re-layouts, body(): pl.pallas_call(kernel, out_shape=jax.ShapeDtypeStruct((COLS, 2 * DH), BF1...  1.74 us

profile of v2, /device:TPU:1, one launch (start us, length us, event | category | flops | bytes accessed | tf_op | source)
XLA Modules:
  0.0 61.0 jit_solution(283165458116526982)
XLA Ops:
  0.0 59.3 %msa_layer.1 = bf16[256,384]{1,0:T(8,128)(2,1)} custom-call(s32[2,256]{1,0:T(2,128)} %ids_hbm.1, s32[2]{0:T(128)} %mask_hbm.1, bf16[33,768]{1,0:T(8,128)(2,1)} %embed_hbm.1, bf16[3,192,768]{2,1,0:T(8,128)(2,1)} %rqkv_hbm.1, bf16[192,768]{1,0:T(8,128)(2,1)} %rout_hbm.1, bf16[3,192,768]{2,1,0:T(8,128)(2,1)} %cqkv_hbm.1, bf16[192,768]{1,0:T(8,128)(2,1)} %cout_hbm.1), custom_call_target="tpu_custom_call" | custom-call | flops 6000000000 | bytes 4000000 | tf_op jit(solution)/shard_map/msa_layer/pallas_call | solution.py:409
  59.3 1.7 %copy.9 = bf16[256,384]{0,1:T(8,128)(2,1)} copy(bf16[256,384]{1,0:T(8,128)(2,1)} %msa_layer.1) | data formatting | bytes 393216 | tf_op jit(solution)/shard_map/msa_layer/pallas_call | solution.py:409

commit v3 on v2

--- a/solution.py
+++ b/solution.py
@@ -17,6 +17,8 @@
 VH = VOCAB * HP
 FAR_Z = (8, 9, 7, 10, 6, 11, 5, 12, 4, 13, 3, 14, 2, 15, 1)
 FAR_Y = (4, 5, 3, 2, 6, 7, 1)
+NEAR_Z = (-4, 3, -3, 2, -2, 1, -1)
+NCOL = 4
 FAR_X = (2, 1, 3)
 FAR_PLANE = (10, 11, 8, 9, 6, 7, 14, 15, 4, 5, 12, 13, 2, 3, 1, 0)
 MESH = pl.DeviceIdType.MESH
@@ -70,7 +72,7 @@
 
         def run(k):
             gate(self.arrives(k), lambda: self.into(k).wait_recv())
-        self.each(run, keys)
+        self.each(run, self.keys[::-1] if keys is None else keys)
 
     def finish(self):
         def run(k):
@@ -89,7 +91,7 @@
     ids_hbm, mask_hbm, embed_hbm, rqkv_hbm, rout_hbm, cqkv_hbm, cout_hbm,
     out_ref,
     ids_ref, mask_ref, embed_ref, rqkv_ref, cqkv_ref,
-    idbuf, tab, wro, wco, emb_s, sel_s, qt_s, kf_s, vf_s, kx_s, vxt_s, wm_s, sc_s,
+    idbuf, tab, wro, wco, emb_s, sel_s, qt_s, kf_s, vf_s, kx_s, vxt_s, wm_s, vo_s, sc_s,
     mixed_s, ctxs, ctxr, sa, ra, sb,
     zs, zr, ys, yr, ts, tr, ros, ror, rfs, rfr, cos, cor, cfs, cfr, xs, xr, as_, ar, bs, br, ls,
 ):
@@ -102,6 +104,8 @@
     grp = y * NC + core
     half = lax.rem(x, 2)
     col_in = lax.div(x, 2)
+    odd = lax.rem(z, 2)
+    first_z = lax.rem(z + NZ - 4 + odd, NZ)
 
     def seq_at(yy, zz, cc):
         return (yy * NZ + zz) * NC + cc
@@ -190,7 +194,7 @@
     row_out.start()
     col_out = weight(cout_hbm, wco, cos, cor)
 
-    emb_t = emb_s[...].T.astype(BF16)
+    vo_s[:, :, 640:768] = emb_s[...].T.astype(BF16).reshape(NX, DH, 128)
     spot = iota((4 * 256, D), 0)
     goal = lax.div(spot, 256) * DH + lax.rem(spot, 256)
     sel_s[...] = jnp.where(
@@ -236,16 +240,31 @@
     head_of = jnp.where(
         lax.div(iota((D, 640), 0), HEAD_DIM) == lax.rem(iota((D, 640), 1), HP), 1.0, 0.0)
     vxt_s[...] = (dot(vf_s[...].T.astype(BF16), rep) * head_of).astype(BF16)
+    wm_s[VH:640, :] = jnp.zeros((640 - VH, NCOL * ROWS), BF16)
+
+    row_out.receive()
+    fetch[4].wait()
+    vo_s[:, part, 0:640] = dot(wro[:, part, :].reshape(4 * 96, D), vxt_s[...]).astype(BF16).reshape(4, 96, 640)
+    twin = s + 1 - 2 * core
+    row_share = Exchange(
+        lambda k: remote(
+            vo_s.at[:, part, pl.ds(0, 640)], vo_s.at[:, part, pl.ds(0, 640)], rfs.at[k], rfr.at[k], twin, x),
+        lambda k: remote(
+            vo_s.at[:, other, pl.ds(0, 640)], vo_s.at[:, other, pl.ds(0, 640)], rfs.at[k], rfr.at[k], twin, x),
+        (0,))
+    row_share.start()
 
     ids_y.receive()
-    row_share = forward(wro, rfs, rfr)
-    row_out.receive()
-    row_share.start()
 
     words = idbuf[:, 0, :]
     low = lax.bitwise_and(words, 65535).astype(F32)
     high = lax.shift_right_logical(words, 16).astype(F32)
     table = jnp.concatenate([low[0:64], high[0:64], low[64:128], high[64:128]], axis=0)
+    place = iota((ROWS, ROWS), 0)
+    from_z = lax.rem(lax.div(place, 128) * 8 + lax.rem(place, 8) + first_z, NZ)
+    from_row = lax.rem(lax.div(place, 64), 2) * 128 + lax.rem(lax.div(place, 8), 8) * 16 + from_z
+    shuffle = jnp.where(from_row == iota((ROWS, ROWS), 1), 1.0, 0.0).astype(BF16)
+    table = dot(shuffle, table.astype(BF16))
     ids = table[:, 0:COLS].astype(BF16)
     live = table[:, COLS:COLS + 128]
     live2 = jnp.concatenate([live, live], axis=1)
@@ -256,27 +275,27 @@
         return jnp.where(of == jnp.asarray(b, BF16), jnp.asarray(1, BF16), jnp.asarray(0, BF16))
 
     count = jnp.sum(live2, axis=0, keepdims=True)
-    first_col = z * 16 + grp * 2
+    first_col = lax.rem(z, 8) * 32 + grp * NCOL
     token = iota((128, ROWS), 0).astype(F32)
     first_lane = jnp.where(iota((128, 128), 1) == 0, 1.0, 0.0).astype(BF16)
     live_row = dot(first_lane, live.astype(BF16), 1, 1)
     own, own_live = [], []
-    for i in range(2):
+    for i in range(NCOL):
         pick = jnp.where(iota((128, COLS), 1) == first_col + i, 1.0, 0.0).astype(BF16)
         hit = jnp.where(dot(pick, ids, 1, 1) == token, 1.0, 0.0)
         own.append(hit.astype(BF16))
         own_live.append((hit * live_row).astype(BF16))
-    own = jnp.concatenate(own, axis=1)
+    wm_s[640:768, :] = jnp.concatenate(own, axis=1)
     picked = dot(sc_s[...], jnp.concatenate(own_live, axis=1)).astype(BF16)
     sums = [None] * 4
     for b in range(VOCAB):
         left = jnp.concatenate([
-            picked[b * HP:(b + 1) * HP, 0:ROWS], picked[VH + b * HP:VH + (b + 1) * HP, 0:ROWS],
-            picked[b * HP:(b + 1) * HP, ROWS:], picked[VH + b * HP:VH + (b + 1) * HP, ROWS:]], axis=0)
+            picked[at + b * HP:at + (b + 1) * HP, i * ROWS:(i + 1) * ROWS]
+            for at in (0, VH) for i in range(NCOL)], axis=0)
         term = dot(left, onehot(ids, b))
         sums[b % 4] = term if sums[b % 4] is None else sums[b % 4] + term
     tied4 = (sums[0] + sums[1]) + (sums[2] + sums[3])
-    tied = jnp.concatenate([tied4[0:16] + tied4[16:32], tied4[32:48] + tied4[48:64]], axis=0)
+    tied = tied4[0:NCOL * HP] + tied4[NCOL * HP:]
     tied = tied * (HEAD_DIM ** (-0.5) * lax.rsqrt(count))
     top = jnp.max(tied, axis=1, keepdims=True)
     weights = jnp.exp(tied - top)
@@ -284,29 +303,32 @@
 
     for b in range(VOCAB):
         share = dot(probs, onehot(ids_t, b))
-        wm_s[b * HP:(b + 1) * HP, 0:ROWS] = share[0:16].astype(BF16)
-        wm_s[b * HP:(b + 1) * HP, ROWS:2 * ROWS] = share[16:32].astype(BF16)
-
-    fetch[4].wait()
+        for i in range(NCOL):
+            wm_s[b * HP:(b + 1) * HP, i * ROWS:(i + 1) * ROWS] = share[i * HP:(i + 1) * HP].astype(BF16)
+
     fetch[5].wait()
     row_share.receive()
-    row_weight = wro[...].reshape(D, D)
     col_weight = cqkv_ref[...].reshape(3 * DH, D)
-    live_here = live2 > 0.0
-
-    context = dot(vxt_s[:, 0:VH], wm_s[...]).astype(BF16)
-    mixed = dot(row_weight, context) + dot(emb_t, own)
-    for q in range(4):
-        mixed_s[q] = mixed[:, 128 * q:128 * q + 128]
-    proj = dot(col_weight, norm_cols(mixed).astype(BF16))
+    live_here = live > 0.0
+
+    mixed = dot(vo_s[...].reshape(D, D), wm_s[...])
+    near = [mixed[:, i * ROWS:i * ROWS + 128] for i in range(NCOL)]
+    for q in range(NX):
+        pair = near[q // 2 * 2:q // 2 * 2 + 2]
+        at = slice(q % 2 * 64, q % 2 * 64 + 64)
+        mixed_s[q] = jnp.concatenate([pair[0][:, at], pair[1][:, at]], axis=1)
+    normed2 = norm_cols(mixed).astype(BF16)
+    proj = dot(col_weight[DH:], normed2)
+    query = dot(col_weight[:DH], jnp.concatenate(
+        [normed2[:, i * ROWS:i * ROWS + 128] for i in range(NCOL)], axis=1))
+    query = query.astype(BF16) * jnp.asarray(0.125, BF16)
     scores, values = [], []
-    for i in range(2):
+    for i in range(NCOL):
         at = slice(i * ROWS, (i + 1) * ROWS)
-        query = proj[0:DH, at].astype(BF16) * jnp.asarray(0.125, BF16)
-        key = proj[DH:2 * DH, at].astype(BF16)
-        value = proj[2 * DH:3 * DH, at].astype(BF16)
+        key = proj[0:DH, at].astype(BF16)
+        value = proj[DH:2 * DH, at].astype(BF16)
         for h in range(0, DH, HEAD_DIM):
-            scores.append(dot(key[h:h + HEAD_DIM], query[h:h + HEAD_DIM], 0, 0))
+            scores.append(dot(key[h:h + HEAD_DIM], query[h:h + HEAD_DIM, i * 128:i * 128 + 128], 0, 0))
             values.append(value[h:h + HEAD_DIM])
     weighted, totals = [], []
     for score in scores:
@@ -314,11 +336,11 @@
         raw = jnp.exp(score - jnp.max(score, axis=0, keepdims=True))
         totals.append(1.0 / jnp.sum(raw, axis=0, keepdims=True))
         weighted.append(raw.astype(BF16))
-    for q in range(6):
-        got = (dot(values[q], weighted[q]) * totals[q]).astype(BF16)
-        at = slice((q % 3) * HEAD_DIM, (q % 3 + 1) * HEAD_DIM)
-        ctxs[q // 3 * 2, at, :] = got[:, 0:128]
-        ctxs[q // 3 * 2 + 1, at, :] = got[:, 128:256]
+    got = [dot(values[q], weighted[q]) * totals[q] for q in range(3 * NCOL)]
+    for q in range(NX):
+        for h in range(3):
+            pair = [got[(q // 2 * 2 + c) * 3 + h][:, q % 2 * 64:q % 2 * 64 + 64] for c in range(2)]
+            ctxs[q, h * HEAD_DIM:(h + 1) * HEAD_DIM, :] = jnp.concatenate(pair, axis=1).astype(BF16)
     to_slot = Exchange(
         lambda k: remote(ctxs.at[ahead(k)], ctxr.at[x], xs.at[k], xr.at[k], s, ahead(k)),
         lambda k: remote(ctxs.at[ahead(k)], ctxr.at[behind(k)], xs.at[k], xr.at[k], s, ahead(k)),
@@ -333,7 +355,7 @@
     col_share.receive()
     to_slot.receive()
 
-    done = dot(wco[...].reshape(D, D), ctxr[...].reshape(D, 128)) + mixed_s[x]
+    context = ctxr[...].reshape(D, 128)
 
     def a_place(j):
         to_x = lax.rem(x + j // 4, NX)
@@ -344,7 +366,7 @@
         to_x, to_half, to_core = a_place(j)
         k = grp * 2 + col_in
         return remote(
-            sa.at[to_x, to_half * 2 + to_core], ra.at[k], as_.at[j], ar.at[k],
+            sa.at[j // 4, to_half * 2 + to_core], ra.at[k], as_.at[j], ar.at[k],
             seq_at(2 * half + to_half, z, to_core), to_x)
 
     def a_into(j):
@@ -360,36 +382,43 @@
         a_out, a_into, FAR_PLANE,
         lambda j: jnp.logical_not(stays) if j == 0 else None,
         lambda j: jnp.logical_not(stays) if j == 0 else None)
-    for to_x in range(NX):
-        turned = done[DH * to_x:DH * (to_x + 1)].T
-        wide = jnp.concatenate([turned[0:64], turned[64:128]], axis=1).astype(BF16)
+    for step in (2, 1, 3, 0):
+        to_x = lax.rem(x + step, NX)
+        rows = pl.ds(pl.multiple_of(to_x * DH, DH), DH)
+        turned = (dot(wco[to_x], context) + mixed_s[x, rows, :]).T
         for g in range(4):
-            sa[to_x, g] = wide[16 * g:16 * g + 16]
-    to_plane.start()
+            rows_of = [jnp.concatenate([turned[r + g * 8:r + g * 8 + 8], turned[64 + r + g * 8:64 + r + g * 8 + 8]], axis=0)
+                       for r in (0, 32)]
+            sa[step, g] = jnp.concatenate(rows_of, axis=1).astype(BF16)
+        to_plane.start([j for j in FAR_PLANE if j // 4 == step])
 
     @pl.when(stays)
     def _():
-        ra[grp * 2 + col_in] = sa[x, lax.rem(y, 2) * 2 + core]
+        ra[grp * 2 + col_in] = sa[0, lax.rem(y, 2) * 2 + core]
 
     order = iota((256, 256), 0)
-    swap = jnp.where(lax.rem(order, 16) * 16 + lax.div(order, 16) == iota((256, 256), 1), 1.0, 0.0).astype(BF16)
+    swap = jnp.where(lax.rem(order, 32) * 8 + lax.div(order, 32) == iota((256, 256), 1), 1.0, 0.0).astype(BF16)
     to_plane.receive()
 
     sb[...] = dot(swap, ra[...].reshape(256, 384)).astype(BF16)
 
-    def z_rows(at):
-        return pl.ds(pl.multiple_of(at * 16, 16), 16)
-
+    def near_part(step):
+        return pl.ds(pl.multiple_of((step + 4 - odd) * 32, 32), 32)
+
+    def col_part(at):
+        return pl.ds(pl.multiple_of(lax.rem(at, 8) * 32, 32), 32)
+
+    side = 1 - 2 * odd
     to_rows = Exchange(
         lambda k: remote(
-            sb.at[z_rows(lax.rem(z + k, NZ)), :], out_ref.at[z_rows(z), :], bs.at[k], br.at[k],
-            seq_at(y, lax.rem(z + k, NZ), core), x),
+            sb.at[near_part(side * k), :], out_ref.at[col_part(z), :], bs.at[k + 4], br.at[side * k + 4],
+            seq_at(y, lax.rem(z + NZ + side * k, NZ), core), x),
         lambda k: remote(
-            sb.at[z_rows(lax.rem(z + NZ - k, NZ)), :], out_ref.at[z_rows(lax.rem(z + NZ - k, NZ)), :],
-            bs.at[k], br.at[k], seq_at(y, lax.rem(z + k, NZ), core), x),
-        tuple(range(1, NZ)))
+            sb.at[near_part(side * k), :], out_ref.at[col_part(z + NZ - side * k), :], bs.at[k + 4], br.at[side * k + 4],
+            seq_at(y, lax.rem(z + NZ + side * k, NZ), core), x),
+        NEAR_Z)
     to_rows.start()
-    keep = pltpu.make_async_copy(sb.at[z_rows(z), :], out_ref.at[z_rows(z), :], ls.at[7])
+    keep = pltpu.make_async_copy(sb.at[near_part(0), :], out_ref.at[col_part(z), :], ls.at[7])
     keep.start()
 
     ids_z.finish()
@@ -400,15 +429,15 @@
     to_slot.finish()
     to_plane.finish()
     keep.wait()
+    to_rows.finish()
     to_rows.receive()
-    to_rows.finish()
 
 
 def body(ids, pad_mask, embed, row_qkv, row_out, col_qkv, col_out):
     dma = pltpu.SemaphoreType.DMA
     got = pl.pallas_call(
         kernel,
-        out_shape=jax.ShapeDtypeStruct((COLS, 2 * DH), BF16),
+        out_shape=pltpu.VMEM((COLS, 2 * DH), BF16),
         in_specs=[pl.BlockSpec(memory_space=pltpu.HBM)] * 7,
         out_specs=pl.BlockSpec(memory_space=pl.ANY),
         scratch_shapes=[
@@ -428,7 +457,8 @@
             pltpu.VMEM((128, D), F32),
             pltpu.VMEM((VH, D), BF16),
             pltpu.VMEM((D, 640), BF16),
-            pltpu.VMEM((VH, 2 * ROWS), BF16),
+            pltpu.VMEM((D, NCOL * ROWS), BF16),
+            pltpu.VMEM((NX, DH, D), BF16),
             pltpu.VMEM((2 * VH, 128), BF16),
             pltpu.VMEM((4, D, 128), F32),
             pltpu.VMEM((NX, DH, 128), BF16),

time: 61.6 us -> 57.4 us (0.932)
  Pallas kernels: 59.3 us -> 56.4 us
  local copies, waits for them, and re-layouts: 1.74 us -> 0.82 us
    pallas_call x1, Pallas kernels: 59.3 us -> 56.4 us  [body(): pl.pallas_call(kernel, out_shape=pltpu.VMEM((COLS, 2 * DH), BF16), in_spe...]
    pallas_call x1, local copies, waits for them, and re-layouts: 1.74 us -> 0.82 us  [body(): pl.pallas_call(kernel, out_shape=pltpu.VMEM((COLS, 2 * DH), BF16), in_spe...]
where the time goes in v3:
time: 57.4 us; the launch traced here: 57.2 us
  Pallas kernels  56.4 us (98%)
  local copies, waits for them, and re-layouts  0.82 us (1%)
    pallas_call x1, Pallas kernels, body(): pl.pallas_call(kernel, out_shape=pltpu.VMEM((COLS, 2 * DH), BF16), in_spe...  56.4 us

profile of v3, /device:TPU:1, one launch (start us, length us, event | category | flops | bytes accessed | tf_op | source)
XLA Modules:
  0.0 57.2 jit_solution(3094869638225376331)
XLA Ops:
  0.0 56.4 %msa_layer.1 = bf16[256,384]{1,0:T(8,128)(2,1)S(1)} custom-call(s32[2,256]{1,0:T(2,128)} %ids_hbm.1, s32[2]{0:T(128)} %mask_hbm.1, bf16[33,768]{1,0:T(8,128)(2,1)} %embed_hbm.1, bf16[3,192,768]{2,1,0:T(8,128)(2,1)} %rqkv_hbm.1, bf16[192,768]{1,0:T(8,128)(2,1)} %rout_hbm.1, bf16[3,192,768]{2,1,0:T(8,128)(2,1)} %cqkv_hbm.1, bf16[192,768]{1,0:T(8,128)(2,1)} %cout_hbm.1), custom_call_target="tpu_custom_call" | custom-call | flops 6000000000 | bytes 4000000 | tf_op jit(solution)/shard_map/msa_layer/pallas_call | solution.py:438
  56.4 0.8 %copy.9 = bf16[256,384]{0,1:T(8,128)(2,1)} copy(bf16[256,384]{1,0:T(8,128)(2,1)S(1)} %msa_layer.1) | data formatting | bytes 393216 | tf_op jit(solution)/shard_map/msa_layer/pallas_call | solution.py:438

commit v4 on v3

--- a/solution.py
+++ b/solution.py
@@ -15,7 +15,7 @@
 ROWS = 256
 HP = 16
 VH = VOCAB * HP
-FAR_Z = (8, 9, 7, 10, 6, 11, 5, 12, 4, 13, 3, 14, 2, 15, 1)
+DIRECT_Z = (4, -4, 3, -3, 2, -2, 1, -1)
 FAR_Y = (4, 5, 3, 2, 6, 7, 1)
 NEAR_Z = (-4, 3, -3, 2, -2, 1, -1)
 NCOL = 4
@@ -116,9 +116,9 @@
 
     barrier = pltpu.get_barrier_semaphore()
 
-    def greet_line(k, carry):
-        pl.semaphore_signal(barrier, inc=1, device_id=(seq_at(y, lax.rem(z + k, NZ), core), x), device_id_type=MESH)
-        return carry
+    for k in DIRECT_Z:
+        pl.semaphore_signal(
+            barrier, inc=1, device_id=(seq_at(y, lax.rem(z + NZ + k, NZ), core), x), device_id_type=MESH)
 
     def greet_plane(k, carry):
         place = lax.rem(x * 8 + grp + k, 32)
@@ -127,7 +127,6 @@
             barrier, inc=1, device_id=(seq_at(lax.div(pg, NC), z, lax.rem(pg, NC)), px), device_id_type=MESH)
         return carry
 
-    lax.fori_loop(1, NZ, greet_line, 0)
     lax.fori_loop(1, 32, greet_plane, 0)
     fetch = [
         pltpu.make_async_copy(a, b, ls.at[i]) for i, (a, b) in enumerate((
@@ -145,6 +144,28 @@
     idbuf[slot, :, 0:COLS] = ids_ref[0:1, :] + ids_ref[1:2, :] * 65536
     idbuf[slot, :, COLS:COLS + 128] = jnp.zeros((1, 128), jnp.int32) + (m0 + m1 * 65536)
 
+    pl.semaphore_wait(barrier, len(DIRECT_Z) + 31)
+
+    def z_slot(k):
+        return idbuf.at[grp * NZ + lax.rem(z + NZ + k, NZ)]
+
+    def z_seq(k):
+        return seq_at(y, lax.rem(z + NZ + k, NZ), core)
+
+    ids_z = Exchange(
+        lambda k: remote(z_slot(0), z_slot(0), zs.at[k + 4], zr.at[k + 4], z_seq(k), x),
+        lambda k: remote(z_slot(-k), z_slot(-k), zs.at[k + 4], zr.at[k + 4], z_seq(k), x),
+        DIRECT_Z)
+    ids_down = Exchange(
+        lambda k: remote(z_slot(k), z_slot(k), zs.at[8 + k], zr.at[8 + k], z_seq(-4), x),
+        lambda k: remote(z_slot(4 + k), z_slot(4 + k), zs.at[8 + k], zr.at[8 + k], z_seq(-4), x),
+        (4, 3, 2, 1))
+    ids_up = Exchange(
+        lambda k: remote(z_slot(-k), z_slot(-k), zs.at[12 + k], zr.at[12 + k], z_seq(4), x),
+        lambda k: remote(z_slot(-4 - k), z_slot(-4 - k), zs.at[12 + k], zr.at[12 + k], z_seq(4), x),
+        (3, 2, 1))
+    ids_z.start()
+
     fetch[2].wait()
     emb_s[...] = jnp.zeros_like(emb_s)
     emb_s[0:VOCAB, :] = embed_ref[...].astype(F32)
@@ -154,17 +175,6 @@
     for t in range(3):
         tab[x, t * 48:(t + 1) * 48, 0:DH] = dot(normed, rqkv_ref[t], 1, 1).astype(BF16)
 
-    pl.semaphore_wait(barrier, NZ - 1 + 31)
-
-    def z_slot(k):
-        return idbuf.at[grp * NZ + lax.rem(z + NZ - k, NZ)]
-
-    ids_z = Exchange(
-        lambda k: remote(idbuf.at[slot], idbuf.at[slot], zs.at[k], zr.at[k], seq_at(y, lax.rem(z + k, NZ), core), x),
-        lambda k: remote(z_slot(k), z_slot(k), zs.at[k], zr.at[k], seq_at(y, lax.rem(z + k, NZ), core), x),
-        FAR_Z)
-    ids_z.start()
-
     part = pl.ds(pl.multiple_of(core * 96, 96), 96)
     other = pl.ds(pl.multiple_of((1 - core) * 96, 96), 96)
     ahead = lambda k: lax.rem(x + k, NX)
@@ -200,7 +210,13 @@
     sel_s[...] = jnp.where(
         jnp.logical_and(goal == iota((4 * 256, D), 1), lax.rem(spot, 256) < DH), 1.0, 0.0).astype(BF16)
 
-    ids_z.receive()
+    ids_z.receive((1, 2, 3))
+    ids_up.start()
+    ids_z.receive((-1, -2, -3, -4))
+    ids_down.start()
+    ids_z.receive((4,))
+    ids_up.receive()
+    ids_down.receive()
     mine = pl.ds(grp * NZ, NZ)
 
     def y_seq(k):
@@ -299,10 +315,11 @@
     tied = tied * (HEAD_DIM ** (-0.5) * lax.rsqrt(count))
     top = jnp.max(tied, axis=1, keepdims=True)
     weights = jnp.exp(tied - top)
-    probs = (weights / jnp.sum(weights, axis=1, keepdims=True)).astype(BF16)
+    scale = 1.0 / jnp.sum(weights, axis=1, keepdims=True)
+    weights = weights.astype(BF16)
 
     for b in range(VOCAB):
-        share = dot(probs, onehot(ids_t, b))
+        share = dot(weights, onehot(ids_t, b)) * scale
         for i in range(NCOL):
             wm_s[b * HP:(b + 1) * HP, i * ROWS:(i + 1) * ROWS] = share[i * HP:(i + 1) * HP].astype(BF16)
 
@@ -422,6 +439,8 @@
     keep.start()
 
     ids_z.finish()
+    ids_up.finish()
+    ids_down.finish()
     ids_y.finish()
     tabs.finish()
     for weights_sent in (row_out, col_out, row_share, col_share):

time: 57.4 us -> 55.8 us (0.972)
  Pallas kernels: 56.4 us -> 54.9 us
    pallas_call x1, Pallas kernels: 56.4 us -> 54.9 us  [body(): pl.pallas_call(kernel, out_shape=pltpu.VMEM((COLS, 2 * DH), BF16), in_spe...]
where the time goes in v4:
time: 55.8 us; the launch traced here: 55.7 us
  Pallas kernels  54.9 us (98%)
  local copies, waits for them, and re-layouts  0.82 us (1%)
    pallas_call x1, Pallas kernels, body(): pl.pallas_call(kernel, out_shape=pltpu.VMEM((COLS, 2 * DH), BF16), in_spe...  54.9 us

profile of v4, /device:TPU:1, one launch (start us, length us, event | category | flops | bytes accessed | tf_op | source)
XLA Modules:
  0.0 55.7 jit_solution(17955353024042899242)
XLA Ops:
  0.0 54.9 %msa_layer.1 = bf16[256,384]{1,0:T(8,128)(2,1)S(1)} custom-call(s32[2,256]{1,0:T(2,128)} %ids_hbm.1, s32[2]{0:T(128)} %mask_hbm.1, bf16[33,768]{1,0:T(8,128)(2,1)} %embed_hbm.1, bf16[3,192,768]{2,1,0:T(8,128)(2,1)} %rqkv_hbm.1, bf16[192,768]{1,0:T(8,128)(2,1)} %rout_hbm.1, bf16[3,192,768]{2,1,0:T(8,128)(2,1)} %cqkv_hbm.1, bf16[192,768]{1,0:T(8,128)(2,1)} %cout_hbm.1), custom_call_target="tpu_custom_call" | custom-call | flops 6000000000 | bytes 4000000 | tf_op jit(solution)/shard_map/msa_layer/pallas_call | solution.py:457
  54.9 0.8 %copy.9 = bf16[256,384]{0,1:T(8,128)(2,1)} copy(bf16[256,384]{1,0:T(8,128)(2,1)S(1)} %msa_layer.1) | data formatting | bytes 393216 | tf_op jit(solution)/shard_map/msa_layer/pallas_call | solution.py:457

commit v5 on v4

--- a/solution.py
+++ b/solution.py
@@ -114,6 +114,13 @@
         return pltpu.make_async_remote_copy(
             src_ref=src, dst_ref=dst, send_sem=ss, recv_sem=rs, device_id=(to_s, to_x), device_id_type=MESH)
 
+    fetch = [
+        pltpu.make_async_copy(a, b, ls.at[i]) for i, (a, b) in enumerate((
+            (ids_hbm, ids_ref), (mask_hbm, mask_ref), (embed_hbm, embed_ref), (rqkv_hbm, rqkv_ref),
+            (rout_hbm, wro.at[x]), (cqkv_hbm, cqkv_ref), (cout_hbm, wco.at[x])))
+    ]
+    fetch[0].start()
+    fetch[1].start()
     barrier = pltpu.get_barrier_semaphore()
 
     for k in DIRECT_Z:
@@ -128,12 +135,7 @@
         return carry
 
     lax.fori_loop(1, 32, greet_plane, 0)
-    fetch = [
-        pltpu.make_async_copy(a, b, ls.at[i]) for i, (a, b) in enumerate((
-            (ids_hbm, ids_ref), (mask_hbm, mask_ref), (embed_hbm, embed_ref), (rqkv_hbm, rqkv_ref),
-            (rout_hbm, wro.at[x]), (cqkv_hbm, cqkv_ref), (cout_hbm, wco.at[x])))
-    ]
-    for copy in fetch:
+    for copy in fetch[2:]:
         copy.start()
 
     slot = grp * NZ + z
@@ -326,7 +328,7 @@
     fetch[5].wait()
     row_share.receive()
     col_weight = cqkv_ref[...].reshape(3 * DH, D)
-    live_here = live > 0.0
+    live_here = live2 > 0.0
 
     mixed = dot(vo_s[...].reshape(D, D), wm_s[...])
     near = [mixed[:, i * ROWS:i * ROWS + 128] for i in range(NCOL)]
@@ -339,21 +341,31 @@
     query = dot(col_weight[:DH], jnp.concatenate(
         [normed2[:, i * ROWS:i * ROWS + 128] for i in range(NCOL)], axis=1))
     query = query.astype(BF16) * jnp.asarray(0.125, BF16)
-    scores, values = [], []
+    keys, queries, values = [], [], []
     for i in range(NCOL):
         at = slice(i * ROWS, (i + 1) * ROWS)
         key = proj[0:DH, at].astype(BF16)
         value = proj[DH:2 * DH, at].astype(BF16)
         for h in range(0, DH, HEAD_DIM):
-            scores.append(dot(key[h:h + HEAD_DIM], query[h:h + HEAD_DIM, i * 128:i * 128 + 128], 0, 0))
+            keys.append(key[h:h + HEAD_DIM])
             values.append(value[h:h + HEAD_DIM])
+            queries.append(query[h:h + HEAD_DIM, i * 128:i * 128 + 128])
+    blank = jnp.zeros((HEAD_DIM, 128), BF16)
+    scores = []
+    for q in range(0, 3 * NCOL, 2):
+        both = jnp.concatenate([
+            jnp.concatenate([queries[q], blank], axis=1), jnp.concatenate([blank, queries[q + 1]], axis=1)], axis=0)
+        scores.append(dot(jnp.concatenate(keys[q:q + 2], axis=0), both, 0, 0))
+    got = []
     weighted, totals = [], []
     for score in scores:
         score = jnp.where(live_here, score, -1e38)
         raw = jnp.exp(score - jnp.max(score, axis=0, keepdims=True))
         totals.append(1.0 / jnp.sum(raw, axis=0, keepdims=True))
         weighted.append(raw.astype(BF16))
-    got = [dot(values[q], weighted[q]) * totals[q] for q in range(3 * NCOL)]
+    for q in range(0, 3 * NCOL, 2):
+        both = dot(jnp.concatenate(values[q:q + 2], axis=0), weighted[q // 2]) * totals[q // 2]
+        got += [both[0:HEAD_DIM, 0:128], both[HEAD_DIM:, 128:256]]
     for q in range(NX):
         for h in range(3):
             pair = [got[(q // 2 * 2 + c) * 3 + h][:, q % 2 * 64:q % 2 * 64 + 64] for c in range(2)]

time: 55.8 us -> 55.8 us (level)
  no operation moved by 1% of the time
where the time goes in v5:
time: 55.8 us; the launch traced here: 55.7 us
  Pallas kernels  54.9 us (98%)
  local copies, waits for them, and re-layouts  0.82 us (1%)
    pallas_call x1, Pallas kernels, body(): pl.pallas_call(kernel, out_shape=pltpu.VMEM((COLS, 2 * DH), BF16), in_spe...  54.9 us

profile of v5, /device:TPU:1, one launch (start us, length us, event | category | flops | bytes accessed | tf_op | source)
XLA Modules:
  0.0 55.7 jit_solution(5692500152587477931)
XLA Ops:
  0.0 54.9 %msa_layer.1 = bf16[256,384]{1,0:T(8,128)(2,1)S(1)} custom-call(s32[2,256]{1,0:T(2,128)} %ids_hbm.1, s32[2]{0:T(128)} %mask_hbm.1, bf16[33,768]{1,0:T(8,128)(2,1)} %embed_hbm.1, bf16[3,192,768]{2,1,0:T(8,128)(2,1)} %rqkv_hbm.1, bf16[192,768]{1,0:T(8,128)(2,1)} %rout_hbm.1, bf16[3,192,768]{2,1,0:T(8,128)(2,1)} %cqkv_hbm.1, bf16[192,768]{1,0:T(8,128)(2,1)} %cout_hbm.1), custom_call_target="tpu_custom_call" | custom-call | flops 6000000000 | bytes 4000000 | tf_op jit(solution)/shard_map/msa_layer/pallas_call | solution.py:469
  54.9 0.8 %copy.9 = bf16[256,384]{0,1:T(8,128)(2,1)} copy(bf16[256,384]{1,0:T(8,128)(2,1)S(1)} %msa_layer.1) | data formatting | bytes 393216 | tf_op jit(solution)/shard_map/msa_layer/pallas_call | solution.py:469

commit v6 on v5

--- a/solution.py
+++ b/solution.py
@@ -172,10 +172,11 @@
     emb_s[...] = jnp.zeros_like(emb_s)
     emb_s[0:VOCAB, :] = embed_ref[...].astype(F32)
     normed = norm_rows(emb_s[...]).astype(BF16)[0:48, :]
-    tab[x] = jnp.zeros((144, 256), BF16)
+    tab[x] = jnp.zeros((112, 256), BF16)
     fetch[3].wait()
-    for t in range(3):
-        tab[x, t * 48:(t + 1) * 48, 0:DH] = dot(normed, rqkv_ref[t], 1, 1).astype(BF16)
+    tab[x, :, 0:DH] = jnp.concatenate(
+        [dot(normed, rqkv_ref[t], 1, 1)[0:VOCAB] for t in range(3)] + [jnp.zeros((112 - 3 * VOCAB, DH), F32)],
+        axis=0).astype(BF16)
 
     part = pl.ds(pl.multiple_of(core * 96, 96), 96)
     other = pl.ds(pl.multiple_of((1 - core) * 96, 96), 96)
@@ -239,10 +240,10 @@
     gathered = jnp.concatenate([tab[i] for i in range(NX)], axis=1)
     tables = dot(gathered, sel_s[...])
     qt_s[...] = jnp.zeros_like(qt_s)
-    qt_s[0:48, :] = tables[0:48].astype(BF16)
-    kf_s[...] = tables[48:96]
+    qt_s[0:48, :] = jnp.concatenate([tables[0:VOCAB], jnp.zeros((48 - VOCAB, D), F32)], axis=0).astype(BF16)
+    kf_s[0:VOCAB, :] = tables[VOCAB:2 * VOCAB]
     vf_s[...] = jnp.zeros_like(vf_s)
-    vf_s[0:48, :] = tables[96:144]
+    vf_s[0:VOCAB, :] = tables[2 * VOCAB:3 * VOCAB]
     own_head = jnp.where(iota((HP, D), 0) == lax.div(iota((HP, D), 1), HEAD_DIM), 1.0, 0.0)
 
     def expand(b, carry):
@@ -478,7 +479,7 @@
             pltpu.VMEM((3, DH, D), BF16),
             pltpu.VMEM((3, DH, D), BF16),
             pltpu.VMEM((128, 1, 384), jnp.int32),
-            pltpu.VMEM((NX, 144, 256), BF16),
+            pltpu.VMEM((NX, 112, 256), BF16),
             pltpu.VMEM((NX, DH, D), BF16),
             pltpu.VMEM((NX, DH, D), BF16),
             pltpu.VMEM((128, D), F32),

time: 55.8 us -> 55.6 us (level)
  no operation moved by 1% of the time
where the time goes in v6:
time: 55.6 us; the launch traced here: 55.5 us
  Pallas kernels  54.6 us (98%)
  local copies, waits for them, and re-layouts  0.82 us (1%)
    pallas_call x1, Pallas kernels, body(): pl.pallas_call(kernel, out_shape=pltpu.VMEM((COLS, 2 * DH), BF16), in_spe...  54.6 us

profile of v6, /device:TPU:1, one launch (start us, length us, event | category | flops | bytes accessed | tf_op | source)
XLA Modules:
  0.0 55.5 jit_solution(2955732625414796979)
XLA Ops:
  0.0 54.6 %msa_layer.1 = bf16[256,384]{1,0:T(8,128)(2,1)S(1)} custom-call(s32[2,256]{1,0:T(2,128)} %ids_hbm.1, s32[2]{0:T(128)} %mask_hbm.1, bf16[33,768]{1,0:T(8,128)(2,1)} %embed_hbm.1, bf16[3,192,768]{2,1,0:T(8,128)(2,1)} %rqkv_hbm.1, bf16[192,768]{1,0:T(8,128)(2,1)} %rout_hbm.1, bf16[3,192,768]{2,1,0:T(8,128)(2,1)} %cqkv_hbm.1, bf16[192,768]{1,0:T(8,128)(2,1)} %cout_hbm.1), custom_call_target="tpu_custom_call" | custom-call | flops 6000000000 | bytes 4000000 | tf_op jit(solution)/shard_map/msa_layer/pallas_call | solution.py:470
  54.6 0.8 %copy.9 = bf16[256,384]{0,1:T(8,128)(2,1)} copy(bf16[256,384]{1,0:T(8,128)(2,1)S(1)} %msa_layer.1) | data formatting | bytes 393216 | tf_op jit(solution)/shard_map/msa_layer/pallas_call | solution.py:470
